TPU v7x, 256 devices: a whole 4x4x8 slice. The times are simulated.
256 devices in a mesh: orb: 32 (over y, x, core), aux: 8 (over z).
Axes of the slice: x: 4, y: 4, z: 8, core: 2. Of those that a mesh axis runs over, the one named last changes fastest.
Arguments:
- three_centre: bfloat16 [32, 2048, 4096], P('orb', 'aux'), may hold values from -6 to 6
- occ_blocks: bfloat16 [256, 64, 64], P(('orb', 'aux')), may hold values from -0.75 to 0.75
- virt_blocks: bfloat16 [256, 64, 64], P(('orb', 'aux')), may hold values from -0.75 to 0.75
- occ_list: int32 [256], replicated, may hold values from 0 to 255, each once
- virt_list: int32 [256], replicated, may hold values from 0 to 255, each once
- term_count: int32 [32], replicated, may hold values from 1 to 8, 129 in all
Outputs:
- polarizability: float32 [2048, 2048], P('aux', 'orb')
Inputs may be any that keep to these rules, and one draw needn't show every extreme that they name: `occ_list`: each slot of the list names one density block; every block is named once. `virt_list`: each slot of the list names one density block; every block is named once. `term_count`: some pair has all 8 terms live.
All inputs are finite; a program needn't handle non-finite values.
Results may differ from a plain program's by a relative error of at most 0.004.
Values may be sent and summed in bfloat16 or wider, within the bound.
No kernel may reach another device: no remote copies, remote signals or barrier semaphores. Data moves between devices by JAX's collectives and lax.ppermute only.
A program may use at most 128 MiB of HBM per device.

v0:
```python
import jax
import jax.numpy as jnp
from jax import lax
from jax.sharding import PartitionSpec as P


def term_value(flat_block, occ_block, virt_block, aux_rows, block_width):
    half_image = jnp.dot(flat_block, virt_block, preferred_element_type=jnp.float32)
    half_image = half_image.astype(jnp.bfloat16).reshape(aux_rows, block_width, block_width)
    result = jnp.einsum("ml,pms->pls", occ_block, half_image, preferred_element_type=jnp.float32)
    return result.reshape(aux_rows, block_width * block_width)


def body(three_centre, occ_blocks, virt_blocks, occ_list, virt_list, term_count):
    occ_all, virt_all = (
        lax.all_gather(occ_blocks, ("orb", "aux"), axis=0, tiled=True),
        lax.all_gather(virt_blocks, ("orb", "aux"), axis=0, tiled=True),
    )
    local_block = three_centre[0]
    aux_rows = local_block.shape[0]
    block_width = occ_all.shape[1]
    term_total = occ_list.shape[0] // lax.axis_size("orb")
    pair_index = lax.axis_index("orb")
    zero_image = jnp.zeros((aux_rows, block_width * block_width), jnp.float32)
    live_terms = term_count[pair_index]
    flat_block = local_block.reshape(aux_rows * block_width, block_width)

    def add_term(step_index, running):
        list_index = pair_index * term_total + step_index
        return running + term_value(
            flat_block,
            occ_all[occ_list[list_index]],
            virt_all[virt_list[list_index]],
            aux_rows,
            block_width,
        )

    image_rows = lax.fori_loop(0, live_terms, add_term, zero_image).astype(jnp.bfloat16)
    partial_sums = lax.dot_general(
        image_rows,
        lax.all_gather(local_block, "aux", axis=0, tiled=True),
        (((1,), (1,)), ((), ())),
        preferred_element_type=jnp.float32,
    )
    summed_chi = lax.psum_scatter(partial_sums, "orb", scatter_dimension=1, tiled=True)
    return summed_chi * (0.25 / block_width)


def solution(mesh):
    placed = (
        P("orb", "aux", None),
        P(("orb", "aux"), None, None),
        P(("orb", "aux"), None, None),
        P(),
        P(),
        P(),
    )
    return jax.shard_map(
        body, mesh=mesh, in_specs=placed, out_specs=P("aux", "orb"), check_vma=False
    )
```

profile of v0, /device:TPU:20, one launch (start us, length us, event | category | flops | bytes accessed | tf_op | source)
XLA Modules:
  0.0 558.3 jit_solution(9282021649899965975)
XLA Ops:
  6.5 0.7 all-gather.5.cloned.1.call-update
  7.3 0.0 all-gather.7.cloned.1.call-start
  7.3 0.7 all-gather.7.cloned.1.call-update
  8.0 0.0 copy-start.2
  8.0 0.0 all-gather.9.cloned.1.call-start
  8.1 0.7 all-gather.9.cloned.1.call-update
  8.8 0.0 reduce-scatter.2.cloned.1.call-start
  8.8 6.9 %reshape_squeeze.3 = bf16[16384,64]{1,0:T(8,128)(2,1)} reshape(bf16[1,256,4096]{2,1,0:T(8,128)(2,1)} %param.8) | data formatting | bytes 4194304 | tf_op jit(solution)/shard_map/reshape;squeeze | solution.py:26
  15.7 0.7 dynamic_slice.23
  16.4 111.1 %all-gather.5.cloned.1.call-done = bf16[256,64,64]{2,1,0:T(8,128)(2,1)} async-done(((bf16[1,64,64]{2,1,0:T(8,128)(2,1)}), bf16[256,64,64]{2,1,0:T(8,128)(2,1)}) %all-gather.5.cloned.1.call-update) | async-done | bytes 2097168 | tf_op jit(solution)/shard_map/all_gather | solution.py:17
  127.5 116.0 %all-gather.7.cloned.1.call-done = bf16[256,64,64]{2,1,0:T(8,128)(2,1)} async-done(((bf16[1,64,64]{2,1,0:T(8,128)(2,1)}), bf16[256,64,64]{2,1,0:T(8,128)(2,1)}) %all-gather.7.cloned.1.call-update) | async-done | bytes 2097168 | tf_op jit(solution)/shard_map/all_gather | solution.py:16
  243.6 2.3 broadcast_in_dim.3
  245.9 52.7 %while.12 = (s32[]{:T(128)}, f32[256,4096]{0,1:T(8,128)}, s32[]{:T(128)}, s32[]{:T(128)}, s32[256]{0:T(256)S(1)}, /*index=5*/bf16[256,64,64]{2,1,0:T(8,128)(2,1)...) while((s32[]{:T(128)}, f32[256,4096]{0,1:T(8,128)}, ...), condition=%wide.region_1.0_spmd, body=%wide.region_0.0_spmd.sunk | while | flops 270532608 | bytes 39878920 | solution.py:38
  246.6 0.6 dynamic_slice.38
  249.1 3.8 fusion.21
  252.9 5.5 reshape.13
  258.4 0.6 dynamic_slice.39
  260.7 3.8 convolution_bitcast_fusion.2
  264.5 2.4 copy.18
  266.9 4.9 bitcast_add_fusion.2
  272.5 0.6 dynamic_slice.38
  275.0 3.8 fusion.21
  278.8 5.5 reshape.13
  284.3 0.6 dynamic_slice.39
  286.6 3.8 convolution_bitcast_fusion.2
  290.4 2.4 copy.18
  292.8 4.9 bitcast_add_fusion.2
  298.6 118.2 %all-gather.9.cloned.1.call-done = bf16[1,2048,4096]{2,1,0:T(8,128)(2,1)} async-done(((bf16[1,256,4096]{2,1,0:T(8,128)(2,1)}), bf16[1,2048,4096]{2,1,0:T(8,128)(2,1)}) %all-gather.9.cloned.1.call-update) | async-done | bytes 16777232 | tf_op jit(solution)/shard_map/all_gather | solution.py:41
  416.7 13.0 %fusion.7 = f32[256,2048]{0,1:T(8,128)} fusion(bf16[1,2048,4096]{2,1,0:T(8,128)(2,1)} %all-gather.9.cloned.1.call-done, f32[256,4096]{0,1:T(8,128)} %get-tuple-element.113), kind=kOutput, calls=%fused_computation.10 | convolution fusion | flops 4296015872 | bytes 23068672 | tf_op jit(solution)/shard_map/dot_general | solution.py:39
  429.8 0.0 reduce-scatter.2.cloned.1.call-update
  429.8 120.5 %reduce-scatter.2.cloned.1.call-done = f32[256,64]{0,1:T(8,128)} async-done(((f32[256,2048]{0,1:T(8,128)}), f32[256,64]{0,1:T(8,128)}) %reduce-scatter.2.cloned.1.call-update) | async-done | bytes 65552 | tf_op jit(solution)/shard_map/reduce_scatter | solution.py:45
  550.3 1.5 broadcast_multiply_fusion
  (6 shorter events, 0.0 us)
Async XLA Ops:
  6.5 121.0 %all-gather.5.cloned.1.call-start = ((), (), s32[]{:S(2)}) async-start(), calls=%async_computation.1 | async-start | bytes 4210688 | tf_op jit(solution)/shard_map/all_gather | solution.py:17
  7.3 236.3 %all-gather.7.cloned.1.call-start = ((), (), s32[]{:S(2)}) async-start(), calls=%async_computation.2 | async-start | bytes 4210688 | tf_op jit(solution)/shard_map/all_gather | solution.py:16
  8.0 7.7 %copy-start.2 = (s32[32]{0:T(128)S(1)}, s32[32]{0:T(128)}, u32[]{:S(2)}) copy-start(s32[32]{0:T(128)} %param.13) | copy-start | bytes 388
  8.0 408.7 %all-gather.9.cloned.1.call-start = ((), (), s32[]{:S(2)}) async-start(), calls=%async_computation.4 | async-start | bytes 18874368 | tf_op jit(solution)/shard_map/all_gather | solution.py:41
  8.8 541.5 %reduce-scatter.2.cloned.1.call-start = ((), (), s32[]{:S(2)}) async-start(), calls=%async_computation.3 | async-start | bytes 2162688 | tf_op jit(solution)/shard_map/reduce_scatter | solution.py:45
  8.8 237.1 %copy-start = (s32[256]{0:T(256)S(1)}, s32[256]{0:T(256)}, u32[]{:S(2)}) copy-start(s32[256]{0:T(256)} %param.12) | copy-start | bytes 3076
  8.8 237.1 %copy-start.1 = (s32[256]{0:T(256)S(1)}, s32[256]{0:T(256)}, u32[]{:S(2)}) copy-start(s32[256]{0:T(256)} %param.11) | copy-start | bytes 3076
Sparse Core Ops, SparseCore 0:
  11.0 116.5 all-gather.4
  131.1 112.3 all-gather.6
  245.4 171.3 all-gather.8
  429.9 120.3 reduce-scatter.1
where the time goes:
time: 561 us; the launch traced here: 558 us
  waiting for transfers between devices  468 us (83%)
  matrix products  28.3 us (5%)
  local copies, waits for them, and re-layouts  28.2 us (5%)
  between operations  13.2 us (2%)
  other arithmetic  11.2 us (2%)
  loops' own time  9.42 us (2%)
    reduce_scatter x1, waiting for transfers between devices, body(): lax.psum_scatter(partial_sums, 'orb', scatter_dimension=1, tiled=True)  120 us
    all_gather x1, waiting for transfers between devices, body(): lax.all_gather(local_block, 'aux', axis=0, tiled=True)  118 us
    all_gather x1, waiting for transfers between devices, body(): lax.all_gather(occ_blocks, ('orb', 'aux'), axis=0, tiled=True)  116 us
    all_gather x1, waiting for transfers between devices, body(): lax.all_gather(virt_blocks, ('orb', 'aux'), axis=0, tiled=True)  111 us
    dot_general x1, matrix products, body(): lax.dot_general(image_rows, lax.all_gather(local_block, 'aux', axis=0, ti...  13 us
  transfers between devices with their start and end apart: 4, of which 4 were waited for; matrix products, arithmetic and copies ran while one was open for 10% of the time, Pallas kernels for 0%

commit v1 on v0

v1 whole, which is shorter than its diff:
```python
import jax
import jax.numpy as jnp
from jax import lax
from jax.experimental import pallas as pl
from jax.experimental.pallas import tpu as pltpu
from jax.sharding import Mesh, PartitionSpec as P

TILES = ((0, 0), (0, 1), (0, -1), (-1, 1), (0, -2), (-1, 2), (2, -1), (2, -2))
B = 64
TERMS = 8
F32, BF16 = jnp.float32, jnp.bfloat16
NT = (((1,), (1,)), ((), ()))


def iota(shape, dim):
    return lax.broadcasted_iota(jnp.int32, shape, dim)


def order_kernel(t_ref, o_ref):
    row, col = iota((256, 256), 0), iota((256, 256), 1)
    source = ((row >> 2) & 3) * 64 + (row >> 4) * 4 + (row & 3)
    pick = jnp.where(source == col, 1.0, 0.0).astype(BF16)
    moved = lax.dot_general(pick, t_ref[...], NT, preferred_element_type=F32)
    o_ref[...] = moved.astype(BF16).reshape(16, 1, 16, 256)


def order_rows(block):
    return pl.pallas_call(
        order_kernel,
        grid=(16,),
        in_specs=[pl.BlockSpec((256, 256), lambda i: (0, i))],
        out_specs=pl.BlockSpec((16, 1, 16, 256), lambda i: (0, i, 0, 0)),
        out_shape=jax.ShapeDtypeStruct((16, 16, 16, 256), BF16),
        cost_estimate=pl.CostEstimate(flops=2 * 16 * 256**3, bytes_accessed=2**22, transcendentals=0),
    )(block)


def weight_kernel(b_ref, w1_ref, w2_ref):
    both = b_ref[0]
    occ, virt = both[:, :B], both[:, B:]
    row, col = iota((256, 256), 0), iota((256, 256), 1)
    tall_row, tall_col = iota((256, B), 0), iota((256, B), 1)
    wide_row, wide_col = iota((B, 256), 0), iota((B, 256), 1)

    def one(hit):
        return jnp.where(hit, 1.0, 0.0).astype(BF16)

    left = one((tall_row >> 4) * 4 + (tall_row & 3) == tall_col)
    right = one((wide_col >> 4) * 4 + (wide_col & 3) == wide_row)
    spread = lax.dot_general(left, virt, NT, preferred_element_type=F32).astype(BF16)
    spread = jnp.dot(spread, right, preferred_element_type=F32)
    w1 = jnp.where(((row >> 2) & 3) == ((col >> 2) & 3), spread, 0.0).astype(BF16)
    w1_ref[...] = w1.reshape(16, 1, 16, 256)

    left = one((tall_row >> 2) == tall_col)
    right = one((wide_col >> 2) == wide_row)
    spread = lax.dot_general(left, occ, NT, preferred_element_type=F32).astype(BF16)
    spread = jnp.dot(spread, right, preferred_element_type=F32)
    w2_ref[...] = jnp.where((row & 3) == (col & 3), spread, 0.0).astype(BF16)


def term_weights(blocks):
    return pl.pallas_call(
        weight_kernel,
        grid=(TERMS,),
        in_specs=[pl.BlockSpec((1, B, 2 * B), lambda j: (j, 0, 0))],
        out_specs=[
            pl.BlockSpec((16, 1, 16, 256), lambda j: (0, j, 0, 0)),
            pl.BlockSpec((256, 256), lambda j: (0, j)),
        ],
        out_shape=[
            jax.ShapeDtypeStruct((16, TERMS, 16, 256), BF16),
            jax.ShapeDtypeStruct((256, TERMS * 256), BF16),
        ],
        cost_estimate=pl.CostEstimate(flops=2**27, bytes_accessed=2**21, transcendentals=0),
    )(blocks)


def image_kernel(t_ref, w1_ref, w2_ref, o_ref, half_ref):
    step = pl.program_id(0)

    @pl.when(step < 16)
    def _():
        slab = t_ref[...].reshape(256, 256)
        for g in range(0, 16, 2):
            part = w1_ref[g:g + 2].reshape(2 * TERMS * 16, 256)
            half = jnp.dot(part, slab, preferred_element_type=F32).astype(BF16)
            half_ref[g:g + 2, :, step] = half.reshape(2, TERMS, 16, 256)

    @pl.when(step >= 16)
    def _():
        half = half_ref[step - 16].reshape(TERMS * 256, 256)
        image = jnp.dot(w2_ref[...], half, preferred_element_type=F32)
        o_ref[...] = image.T.astype(BF16)


def image_rows(block, w1, w2):
    return pl.pallas_call(
        image_kernel,
        grid=(32,),
        in_specs=[
            pl.BlockSpec((16, 1, 16, 256), lambda i: (0, jnp.minimum(i, 15), 0, 0)),
            pl.BlockSpec((16, TERMS, 16, 256), lambda i: (0, 0, 0, 0)),
            pl.BlockSpec((256, TERMS * 256), lambda i: (0, 0)),
        ],
        out_specs=pl.BlockSpec((256, 256), lambda i: (0, jnp.maximum(i - 16, 0))),
        out_shape=jax.ShapeDtypeStruct((256, 4096), BF16),
        scratch_shapes=[pltpu.VMEM((16, TERMS, 16, 16, 256), BF16)],
        compiler_params=pltpu.CompilerParams(vmem_limit_bytes=40 * 2**20),
        cost_estimate=pl.CostEstimate(flops=2 * 256 * 256**3, bytes_accessed=6 * 2**20, transcendentals=0),
    )(block, w1, w2)


def tile_kernel(count, i_ref, *refs):
    step = pl.program_id(0)
    o_ref, sum_ref = refs[count], refs[count + 1]
    image = i_ref[...]
    for n in range(count):
        part = jnp.dot(image, refs[n][...].reshape(1024, 256), preferred_element_type=F32)

        @pl.when(step == 0)
        def _():
            sum_ref[n] = part

        @pl.when(step > 0)
        def _():
            sum_ref[n] += part

        @pl.when(step == 3)
        def _():
            o_ref[n] = sum_ref[n].T


def tiles(image, blocks):
    count = len(blocks)

    def kernel(*refs):
        tile_kernel(count, *refs)

    return pl.pallas_call(
        kernel,
        grid=(4,),
        in_specs=[pl.BlockSpec((256, 1024), lambda i: (0, i))]
        + [pl.BlockSpec((4, 16, 16, 256), lambda i: (i, 0, 0, 0))] * count,
        out_specs=pl.BlockSpec((count, 256, 256), lambda i: (0, 0, 0)),
        out_shape=jax.ShapeDtypeStruct((count, 256, 256), F32),
        scratch_shapes=[pltpu.VMEM((count, 256, 256), F32)],
        compiler_params=pltpu.CompilerParams(vmem_limit_bytes=32 * 2**20),
        cost_estimate=pl.CostEstimate(
            flops=2 * count * 4096 * 256**2, bytes_accessed=(count + 1) * 2**21, transcendentals=0
        ),
    )(image, *blocks)


ALL = ("y", "x", "c", "z")
ORB = ("y", "x", "c")
PLACES = [(y, x, c, z) for y in range(4) for x in range(4) for c in range(2) for z in range(8)]


def number(y, x, c, z):
    return ((y * 4 + x) * 2 + c) * 8 + z


def moved(value, target):
    return lax.ppermute(value, ALL, [(number(*p), number(*target(*p))) for p in PLACES])


def up(value):
    return moved(value, lambda y, x, c, z: (y, x, c, (z + 1) % 8))


def down(value):
    return moved(value, lambda y, x, c, z: (y, x, c, (z + 7) % 8))


def spread_z(block):
    return lax.all_to_all(jnp.broadcast_to(block[None], (8,) + block.shape), "z", 0, 0)


def pair_blocks(occ_block, virt_block, occ_list, virt_list, term_count):
    pair, z = lax.axis_index(ORB), lax.axis_index("z")
    column = spread_z(jnp.concatenate([occ_block, virt_block], axis=1))
    slots = (occ_list.reshape(32, 8), virt_list.reshape(32, 8))
    wanted = [lax.dynamic_index_in_dim(s, z, 1, keepdims=False)[:, None, None] for s in slots]
    wanted = jnp.where(iota((1, 1, 2 * B), 2) < B, wanted[0], wanted[1]) - pair * 8
    outgoing = jnp.zeros((32, B, 2 * B), BF16)
    for r in range(8):
        outgoing = jnp.where(wanted == r, column[r][None], outgoing)
    arrived = lax.all_to_all(outgoing, ORB, 0, 0)
    mine = arrived.astype(F32).sum(0).astype(BF16)
    mine = jnp.where(z < term_count[pair], mine, jnp.zeros_like(mine))
    return spread_z(mine)


def final_place(y, x, c, z):
    row, col = TILES[c * 4 + y]
    orb = ((z + col) % 8) * 4 + x
    return (orb // 8, orb // 2 % 4, orb % 2, (z + row) % 8)


def body(three_centre, occ_blocks, virt_blocks, occ_list, virt_list, term_count):
    held = {0: order_rows(three_centre[0])}
    held[-1], held[1] = up(held[0]), down(held[0])
    held[-2], held[2] = up(held[-1]), down(held[1])
    blocks = pair_blocks(occ_blocks[0], virt_blocks[0], occ_list, virt_list, term_count)
    w1, w2 = term_weights(blocks)
    image = {0: image_rows(held[0], w1, w2)}
    first = tiles(image[0], [held[0], held[1], held[-1]])
    image[-1] = image_rows(held[-1], w1, w2)
    second = tiles(image[-1], [held[1]])
    third = tiles(image[0], [held[-2]])
    fourth = tiles(image[-1], [held[2]])
    image[2] = image_rows(held[2], w1, w2)
    fifth = tiles(image[2], [held[-1], held[-2]])
    core = lax.axis_index("c")
    low = jnp.concatenate([first, second], axis=0)
    high = jnp.concatenate([third, fourth, fifth], axis=0)
    kept, sent = jnp.where(core == 0, low, high), jnp.where(core == 0, high, low)
    total = kept + moved(sent, lambda y, x, c, z: (y, x, 1 - c, z))
    total = lax.all_to_all(total, "y", 0, 0).sum(0)
    total = lax.all_to_all(total.reshape(4, B, 256), "x", 0, 0).sum(0)
    return moved(total * (0.25 / B), final_place).T


def solution(mesh):
    fine = Mesh(mesh.devices.reshape(4, 4, 2, 8), ALL)
    spread = P(ALL, None, None)
    placed = (P(ORB, "z", None), spread, spread, P(), P(), P())
    return jax.shard_map(body, mesh=fine, in_specs=placed, out_specs=P("z", ORB), check_vma=False)
```

time: 561 us -> 265 us (0.47)
  waiting for transfers between devices: 468 us -> 106 us
  Pallas kernels: 0 us -> 89.8 us
  matrix products: 28.3 us -> 0 us
  starting transfers between devices: 0.12 us -> 27.9 us
  blocking collectives: 0 us -> 26.6 us
  local copies, waits for them, and re-layouts: 28.2 us -> 7.62 us
  between operations: 13.2 us -> 0.9 us
  loops' own time: 9.42 us -> 0 us
  other arithmetic: 11.2 us -> 1.83 us
    all_gather x3 -> x0, waiting for transfers between devices: 345 us -> none  [the longest x1 118 us: body(): lax.all_gather(local_block, 'aux', axis=0, tiled=True)]
    reduce_scatter x1 -> x0, waiting for transfers between devices: 120 us -> none  [body(): lax.psum_scatter(partial_sums, 'orb', scatter_dimension=1, tiled=True)]
    all_to_all x0 -> x3, waiting for transfers between devices: none -> 98.3 us  [the longest x2 91.5 us: spread_z(): lax.all_to_all(jnp.broadcast_to(block[None], (8,) + block.shape), 'z', 0, 0)]
    pallas_call x0 -> x10, Pallas kernels: none -> 89.8 us  [the longest x3 53.3 us: image_rows(): pl.pallas_call(image_kernel, grid=(32,), in_specs=[pl.BlockSpec((16, 1, 1...]
    dot_general x5 -> x0, matrix products: 28.3 us -> none  [the longest x1 13 us: body(): lax.dot_general(image_rows, lax.all_gather(local_block, 'aux', axis=0, ti...]
    all_to_all x0 -> x2, blocking collectives: none -> 26.6 us  [the longest x1 17.5 us: body(): total = lax.all_to_all(total, 'y', 0, 0).sum(0)]
    all_to_all x0 -> x3, starting transfers between devices: none -> 16.6 us  [the longest x2 9.18 us: spread_z(): lax.all_to_all(jnp.broadcast_to(block[None], (8,) + block.shape), 'z', 0, 0)]
    ppermute x0 -> x6, starting transfers between devices: none -> 11.4 us  [moved(): lax.ppermute(value, ALL, [(number(*p), number(*target(*p))) for p in PLAC...]
  transfers between devices with their start and end apart: 4 -> 9, of which waited for: 4 -> 5; matrix products, arithmetic and copies ran while one was open for 10% -> 1% of each run, Pallas kernels for 0% -> 28%
where the time goes in v1:
time: 265 us; the launch traced here: 261 us
  waiting for transfers between devices  106 us (40%)
  Pallas kernels  89.8 us (34%)
  starting transfers between devices  27.9 us (11%)
  blocking collectives  26.6 us (10%)
  local copies, waits for them, and re-layouts  7.62 us (3%)
    all_to_all x2, waiting for transfers between devices, spread_z(): lax.all_to_all(jnp.broadcast_to(block[None], (8,) + block.shape), 'z', 0, 0)  91.5 us
    pallas_call x3, Pallas kernels, image_rows(): pl.pallas_call(image_kernel, grid=(32,), in_specs=[pl.BlockSpec((16, 1, 1...  53.3 us
    pallas_call x5, Pallas kernels, tiles(): pl.pallas_call(kernel, grid=(4,), in_specs=[pl.BlockSpec((256, 1024), lam...  18.9 us
    all_to_all x1, blocking collectives, body(): total = lax.all_to_all(total, 'y', 0, 0).sum(0)  17.5 us
    ppermute x6, starting transfers between devices, moved(): lax.ppermute(value, ALL, [(number(*p), number(*target(*p))) for p in PLAC...  11.4 us
    pallas_call x1, Pallas kernels, order_rows(): pl.pallas_call(order_kernel, grid=(16,), in_specs=[pl.BlockSpec((256, 256...  10.9 us
    all_to_all x2, starting transfers between devices, spread_z(): lax.all_to_all(jnp.broadcast_to(block[None], (8,) + block.shape), 'z', 0, 0)  9.18 us
    all_to_all x1, blocking collectives, body(): total = lax.all_to_all(total.reshape(4, B, 256), 'x', 0, 0).sum(0)  9.07 us
  transfers between devices with their start and end apart: 9, of which 5 were waited for; matrix products, arithmetic and copies ran while one was open for 1% of the time, Pallas kernels for 28%

profile of v1, /device:TPU:20, one launch (start us, length us, event | category | flops | bytes accessed | tf_op | source)
XLA Modules:
  0.0 260.9 jit_solution(1552884847732482559)
XLA Ops:
  0.0 10.9 %shard_map.64.t_ref.refs_1_ = bf16[16,16,16,256]{3,2,1,0:T(8,128)(2,1)} custom-call(bf16[256,4096]{1,0:T(8,128)(2,1)} %bitcast.22), custom_call_target="tpu_custom_call" | custom-call | flops 536870912 | bytes 4194304 | tf_op jit(solution)/shard_map/pallas_call | solution.py:28
  11.0 5.9 %collective-permute-start = (bf16[16,16,16,256]{3,2,1,0:T(8,128)(2,1)}, bf16[16,16,16,256]{3,2,1,0:T(8,128)(2,1)}, u32[]{:S(2)}, u32[]{:S(2)}) collective-permute-start(bf16[16,16,16,256]{3,2,1,0:T(8,128)(2,1)} %shard_map.64.t_ref.refs_1_), channel_id=1, source_target_pairs={{0,7},{1,0},{2,1},{3,2},{4,3},{5,4},{6,5},{7,6},{8,15},{9,8},{10,9... | collective-permute-start | bytes 6291464 | tf_op jit(solution)/shard_map/ppermute | solution.py:165
  16.9 0.7 broadcast_in_dim.156
  17.6 4.6 %all-to-all-start = ((bf16[8,64,128]{2,1,0:T(8,128)(2,1)}), bf16[8,64,128]{2,1,0:T(8,128)(2,1)S(1)}, u32[]{:S(2)}, u32[]{:S(2)}) async-start(bf16[8,64,128]{2,1,0:T(8,128)(2,1)} %broadcast_in_dim.156), calls=%async_computation | async-start | bytes 262144 | tf_op jit(solution)/shard_map/all_to_all | solution.py:177
  22.7 45.4 %all-to-all-done = bf16[8,64,128]{2,1,0:T(8,128)(2,1)S(1)} async-done(((bf16[8,64,128]{2,1,0:T(8,128)(2,1)}), bf16[8,64,128]{2,1,0:T(8,128)(2,1)S(1)}, u32[]{:S(2)}, u32[]{:S(2)}) %all-to-all-start) | async-done | bytes 131104 | tf_op jit(solution)/shard_map/all_to_all | solution.py:177
  68.2 1.1 select_select_fusion
  69.3 7.4 %all-to-all-start.1 = ((bf16[32,64,128]{2,1,0:T(8,128)(2,1)}), bf16[32,64,128]{2,1,0:T(8,128)(2,1)S(1)}, u32[]{:S(2)}, u32[]{:S(2)}) async-start(bf16[32,64,128]{2,1,0:T(8,128)(2,1)} %select_select_fusion), calls=%async_computation.1 | async-start | bytes 1048576 | tf_op jit(solution)/shard_map/all_to_all | solution.py:189
  76.7 0.6 dynamic_slice.10
  77.9 6.8 %all-to-all-done.1 = bf16[32,64,128]{2,1,0:T(8,128)(2,1)S(1)} async-done(((bf16[32,64,128]{2,1,0:T(8,128)(2,1)}), bf16[32,64,128]{2,1,0:T(8,128)(2,1)S(1)}, u32[]{:S(2)}, u32[]{:S(2)}) %all-to-all-start.1) | async-done | bytes 524320 | tf_op jit(solution)/shard_map/all_to_all | solution.py:189
  84.9 0.7 broadcast_in_dim.182
  85.5 4.5 %all-to-all-start.2 = ((bf16[8,64,128]{2,1,0:T(8,128)(2,1)}), bf16[8,64,128]{2,1,0:T(8,128)(2,1)S(1)}, u32[]{:S(2)}, u32[]{:S(2)}) async-start(bf16[8,64,128]{2,1,0:T(8,128)(2,1)} %broadcast_in_dim.182), calls=%async_computation.2 | async-start | bytes 262144 | tf_op jit(solution)/shard_map/all_to_all | solution.py:177
  90.1 46.1 %all-to-all-done.2.b_ref = bf16[8,64,128]{2,1,0:T(8,128)(2,1)S(1)} async-done(((bf16[8,64,128]{2,1,0:T(8,128)(2,1)}), bf16[8,64,128]{2,1,0:T(8,128)(2,1)S(1)}, u32[]{:S(2)}, u32[]{:S(2)}) %all-to-all-start.2) | async-done | bytes 131104 | tf_op jit(solution)/shard_map/all_to_all | solution.py:177
  136.2 0.6 copy-done.4
  136.9 6.7 %shard_map.65 = (bf16[16,8,16,256]{3,2,1,0:T(8,128)(2,1)}, bf16[256,2048]{1,0:T(8,128)(2,1)}) custom-call(bf16[8,64,128]{2,1,0:T(8,128)(2,1)} %copy-done.4), custom_call_target="tpu_custom_call" | custom-call | flops 134217728 | bytes 2097152 | tf_op jit(solution)/shard_map/pallas_call | solution.py:63
  143.5 0.4 collective-permute-start.2
  143.9 1.6 copy-done
  145.5 1.2 copy-done.2
  146.7 1.2 copy-done.3
  148.0 16.4 %shard_map.66.refs_0_ = bf16[256,4096]{1,0:T(8,128)(2,1)S(1)} custom-call(bf16[16,16,16,256]{3,2,1,0:T(8,128)(2,1)S(1)} %copy-done, bf16[16,8,16,256]{3,2,1,0:T(8,128)(2,1)S(1)} %copy-done.2, bf16[256,2048]{1,0:T(8,128)(2,1)S(1)} %copy-done.3), custom_call_target="tpu_custom_call" | custom-call | flops 8589934592 | bytes 6291456 | tf_op jit(solution)/shard_map/pallas_call | solution.py:98
  164.4 16.4 %shard_map.68.refs_0_ = bf16[256,4096]{1,0:T(8,128)(2,1)S(1)} custom-call(bf16[16,16,16,256]{3,2,1,0:T(8,128)(2,1)S(1)} %collective-permute-done.1.refs_3_.t_ref.refs_1_, bf16[16,8,16,256]{3,2,1,0:T(8,128)(2,1)S(1)} %copy-done.2, bf16[256,2048]{1,0:T(8,128)(2,1)S(1)} %copy-done.3), custom_call_target="tpu_custom_call" | custom-call | flops 8589934592 | bytes 6291456 | tf_op jit(solution)/shard_map/pallas_call | solution.py:98
  180.8 3.5 %shard_map.69 = f32[1,256,256]{2,1,0:T(8,128)S(1)} custom-call(bf16[256,4096]{1,0:T(8,128)(2,1)S(1)} %shard_map.68.refs_0_, bf16[16,16,16,256]{3,2,1,0:T(8,128)(2,1)} %collective-permute-done.refs_2_.refs_1_), custom_call_target="tpu_custom_call" | custom-call | flops 536870912 | bytes 4194304 | tf_op jit(solution)/shard_map/pallas_call | solution.py:140
  184.3 6.4 %shard_map.67 = f32[3,256,256]{2,1,0:T(8,128)S(1)} custom-call(bf16[256,4096]{1,0:T(8,128)(2,1)S(1)} %shard_map.66.refs_0_, bf16[16,16,16,256]{3,2,1,0:T(8,128)(2,1)S(1)} %copy-done.1, bf16[16,16,16,256]{3,2,1,0:T(8,128)(2,1)} %collective-permute-done.refs_2_.refs_1_, bf16[16,16,16,256]{3,2,1,0:T(8,128)(2,1)S(1)} %collective-permute-done.1.refs_3_.t_ref.refs_1_), custom_call_target="tpu_custom_call" | custom-call | flops 1610612736 | bytes 8388608 | tf_op jit(solution)/shard_map/pallas_call | solution.py:140
  190.7 3.4 %shard_map.71 = f32[1,256,256]{2,1,0:T(8,128)S(1)} custom-call(bf16[256,4096]{1,0:T(8,128)(2,1)S(1)} %shard_map.68.refs_0_, bf16[16,16,16,256]{3,2,1,0:T(8,128)(2,1)} %collective-permute-done.3.refs_1_.t_ref), custom_call_target="tpu_custom_call" | custom-call | flops 536870912 | bytes 4194304 | tf_op jit(solution)/shard_map/pallas_call | solution.py:140
  194.1 20.5 %shard_map.72.refs_0_ = bf16[256,4096]{1,0:T(8,128)(2,1)S(1)} custom-call(bf16[16,16,16,256]{3,2,1,0:T(8,128)(2,1)} %collective-permute-done.3.refs_1_.t_ref, bf16[16,8,16,256]{3,2,1,0:T(8,128)(2,1)S(1)} %copy-done.2, bf16[256,2048]{1,0:T(8,128)(2,1)S(1)} %copy-done.3), custom_call_target="tpu_custom_call" | custom-call | flops 8589934592 | bytes 6291456 | tf_op jit(solution)/shard_map/pallas_call | solution.py:98
  214.6 1.6 shard_map.70
  216.3 4.0 %shard_map.73 = f32[2,256,256]{2,1,0:T(8,128)S(1)} custom-call(bf16[256,4096]{1,0:T(8,128)(2,1)S(1)} %shard_map.72.refs_0_, bf16[16,16,16,256]{3,2,1,0:T(8,128)(2,1)S(1)} %collective-permute-done.1.refs_3_.t_ref.refs_1_, bf16[16,16,16,256]{3,2,1,0:T(8,128)(2,1)S(1)} %collective-permute-done.2.refs_1_.refs_2_), custom_call_target="tpu_custom_call" | custom-call | flops 1073741824 | bytes 6291456 | tf_op jit(solution)/shard_map/pallas_call | solution.py:140
  220.5 2.6 %collective-permute-done.4 = f32[4,256,256]{2,1,0:T(8,128)S(1)} collective-permute-done((f32[4,256,256]{2,1,0:T(8,128)S(1)}, f32[4,256,256]{2,1,0:T(8,128)S(1)}, u32[]{:S(2)}, u32[]{:S(2)}) %collective-permute-start.4) | collective-permute-done | bytes 1048608 | tf_op jit(solution)/shard_map/ppermute | solution.py:165
  223.3 17.5 %all_to_all.25 = f32[4,256,256]{2,1,0:T(8,128)S(1)} all-to-all(f32[4,256,256]{2,1,0:T(8,128)S(1)} %select_add_fusion), channel_id=1, replica_groups=mesh['y'=4,'x'=4,'c'=2,'z'=8] {'y'}, dimensions={0} | all-to-all | bytes 2097152 | tf_op jit(solution)/shard_map/all_to_all | solution.py:220
  241.0 9.1 %all_to_all.26 = f32[4,64,256]{2,1,0:T(8,128)S(1)} all-to-all(f32[4,64,256]{2,1,0:T(8,128)S(1)} %bitcast.23), channel_id=1, replica_groups=mesh['y'=4,'x'=4,'c'=2,'z'=8] {'x'}, dimensions={0} | all-to-all | bytes 524288 | tf_op jit(solution)/shard_map/all_to_all | solution.py:221
  250.1 5.0 %collective-permute-start.5 = (f32[64,256]{1,0:T(8,128)S(1)}, f32[64,256]{1,0:T(8,128)S(1)}, u32[]{:S(2)}, u32[]{:S(2)}) collective-permute-start(f32[64,256]{1,0:T(8,128)S(1)} %broadcast_multiply_fusion), channel_id=1, source_target_pairs={{0,0},{1,33},{2,66},{3,99},{4,132},{5,165},{6,198},{7,231},{8,192}... | collective-permute-start | bytes 196616 | tf_op jit(solution)/shard_map/ppermute | solution.py:165
  255.0 5.2 %collective-permute-done.5 = f32[64,256]{1,0:T(8,128)S(1)} collective-permute-done((f32[64,256]{1,0:T(8,128)S(1)}, f32[64,256]{1,0:T(8,128)S(1)}, u32[]{:S(2)}, u32[]{:S(2)}) %collective-permute-start.5) | collective-permute-done | bytes 65568 | tf_op jit(solution)/shard_map/ppermute | solution.py:165
  260.3 0.6 copy.8
  (37 shorter events, 1.3 us)
Async XLA Ops:
  0.0 16.8 %copy-start.5 = (bf16[1,64,64]{2,1,0:T(8,128)(2,1)S(1)}, bf16[1,64,64]{2,1,0:T(8,128)(2,1)}, u32[]{:S(2)}) copy-start(bf16[1,64,64]{2,1,0:T(8,128)(2,1)} %param.8) | copy-start | bytes 24580
  0.0 16.8 %copy-start.6 = (bf16[1,64,64]{2,1,0:T(8,128)(2,1)S(1)}, bf16[1,64,64]{2,1,0:T(8,128)(2,1)}, u32[]{:S(2)}) copy-start(bf16[1,64,64]{2,1,0:T(8,128)(2,1)} %param.7) | copy-start | bytes 24580
  0.0 22.2 %copy-start.7 = (s32[256]{0:T(256)S(1)}, s32[256]{0:T(256)}, u32[]{:S(2)}) copy-start(s32[256]{0:T(256)} %param.10) | copy-start | bytes 3076
  0.0 22.3 %copy-start.8 = (s32[256]{0:T(256)S(1)}, s32[256]{0:T(256)}, u32[]{:S(2)}) copy-start(s32[256]{0:T(256)} %param.9) | copy-start | bytes 3076
  11.0 65.7 %copy-start.9 = (s32[32]{0:T(128)S(1)}, s32[32]{0:T(128)}, u32[]{:S(2)}) copy-start(s32[32]{0:T(128)} %param.11) | copy-start | bytes 388
  11.0 73.8 %collective-permute-start = (bf16[16,16,16,256]{3,2,1,0:T(8,128)(2,1)}, bf16[16,16,16,256]{3,2,1,0:T(8,128)(2,1)}, u32[]{:S(2)}, u32[]{:S(2)}) collective-permute-start(bf16[16,16,16,256]{3,2,1,0:T(8,128)(2,1)} %shard_map.64.t_ref.refs_1_), channel_id=1, source_target_pairs={{0,7},{1,0},{2,1},{3,2},{4,3},{5,4},{6,5},{7,6},{8,15},{9,8},{10,9... | collective-permute-start | bytes 6291464 | tf_op jit(solution)/shard_map/ppermute | solution.py:165
  16.8 126.7 %collective-permute-start.1 = (bf16[16,16,16,256]{3,2,1,0:T(8,128)(2,1)}, bf16[16,16,16,256]{3,2,1,0:T(8,128)(2,1)S(1)}, u32[]{:S(2)}, u32[]{:S(2)}) collective-permute-start(bf16[16,16,16,256]{3,2,1,0:T(8,128)(2,1)} %shard_map.64.t_ref.refs_1_), channel_id=1, source_target_pairs={{0,1},{1,2},{2,3},{3,4},{4,5},{5,6},{6,7},{7,0},{8,9},{9,10},{10,1... | collective-permute-start | bytes 6291464 | tf_op jit(solution)/shard_map/ppermute | solution.py:165
  17.6 50.6 %all-to-all-start = ((bf16[8,64,128]{2,1,0:T(8,128)(2,1)}), bf16[8,64,128]{2,1,0:T(8,128)(2,1)S(1)}, u32[]{:S(2)}, u32[]{:S(2)}) async-start(bf16[8,64,128]{2,1,0:T(8,128)(2,1)} %broadcast_in_dim.156), calls=%async_computation | async-start | bytes 262144 | tf_op jit(solution)/shard_map/all_to_all | solution.py:177
  69.3 15.4 %all-to-all-start.1 = ((bf16[32,64,128]{2,1,0:T(8,128)(2,1)}), bf16[32,64,128]{2,1,0:T(8,128)(2,1)S(1)}, u32[]{:S(2)}, u32[]{:S(2)}) async-start(bf16[32,64,128]{2,1,0:T(8,128)(2,1)} %select_select_fusion), calls=%async_computation.1 | async-start | bytes 1048576 | tf_op jit(solution)/shard_map/all_to_all | solution.py:189
  84.8 105.9 %collective-permute-start.3 = (bf16[16,16,16,256]{3,2,1,0:T(8,128)(2,1)}, bf16[16,16,16,256]{3,2,1,0:T(8,128)(2,1)}, u32[]{:S(2)}, u32[]{:S(2)}) collective-permute-start(bf16[16,16,16,256]{3,2,1,0:T(8,128)(2,1)} %collective-permute-done.refs_2_.refs_1_), channel_id=1, source_target_pairs={{0,7},{1,0},{2,1},{3,2},{4,3},{5,4},{6,5},{7,6},{8,15},{9,8},{10,9... | collective-permute-start | bytes 6291464 | tf_op jit(solution)/shard_map/ppermute | solution.py:165
  85.5 50.7 %all-to-all-start.2 = ((bf16[8,64,128]{2,1,0:T(8,128)(2,1)}), bf16[8,64,128]{2,1,0:T(8,128)(2,1)S(1)}, u32[]{:S(2)}, u32[]{:S(2)}) async-start(bf16[8,64,128]{2,1,0:T(8,128)(2,1)} %broadcast_in_dim.182), calls=%async_computation.2 | async-start | bytes 262144 | tf_op jit(solution)/shard_map/all_to_all | solution.py:177
  136.2 0.7 copy-start.4
  143.5 71.1 %collective-permute-start.2 = (bf16[16,16,16,256]{3,2,1,0:T(8,128)(2,1)S(1)}, bf16[16,16,16,256]{3,2,1,0:T(8,128)(2,1)S(1)}, u32[]{:S(2)}, u32[]{:S(2)}) collective-permute-start(bf16[16,16,16,256]{3,2,1,0:T(8,128)(2,1)S(1)} %collective-permute-done.1.refs_3_.t_ref.refs_1_), channel_id=1, source_target_pairs={{0,1},{1,2},{2,3},{3,4},{4,5},{5,6},{6,7},{7,0},{8,9},{9,10},{10,1... | collective-permute-start | bytes 6291464 | tf_op jit(solution)/shard_map/ppermute | solution.py:165
  143.9 1.6 copy-start
  145.5 1.2 copy-start.2
  146.7 1.2 copy-start.3
  180.8 3.5 %copy-start.1 = (bf16[16,16,16,256]{3,2,1,0:T(8,128)(2,1)S(1)}, bf16[16,16,16,256]{3,2,1,0:T(8,128)(2,1)}, u32[]{:S(2)}) copy-start(bf16[16,16,16,256]{3,2,1,0:T(8,128)(2,1)} %shard_map.64.t_ref.refs_1_) | copy-start | bytes 6291460
  220.4 2.7 %collective-permute-start.4 = (f32[4,256,256]{2,1,0:T(8,128)S(1)}, f32[4,256,256]{2,1,0:T(8,128)S(1)}, u32[]{:S(2)}, u32[]{:S(2)}) collective-permute-start(f32[4,256,256]{2,1,0:T(8,128)S(1)} %fusion), channel_id=1, source_target_pairs={{0,8},{1,9},{2,10},{3,11},{4,12},{5,13},{6,14},{7,15},{8,0},{9,1},... | collective-permute-start | bytes 3145736 | tf_op jit(solution)/shard_map/ppermute | solution.py:165
  250.1 10.2 %collective-permute-start.5 = (f32[64,256]{1,0:T(8,128)S(1)}, f32[64,256]{1,0:T(8,128)S(1)}, u32[]{:S(2)}, u32[]{:S(2)}) collective-permute-start(f32[64,256]{1,0:T(8,128)S(1)} %broadcast_multiply_fusion), channel_id=1, source_target_pairs={{0,0},{1,33},{2,66},{3,99},{4,132},{5,165},{6,198},{7,231},{8,192}... | collective-permute-start | bytes 196616 | tf_op jit(solution)/shard_map/ppermute | solution.py:165

commit v2 on v0

v2 whole, which is shorter than its diff:
```python
import jax
import jax.numpy as jnp
from jax import lax
from jax.experimental import pallas as pl
from jax.experimental.pallas import tpu as pltpu
from jax.sharding import Mesh, PartitionSpec as P

EARLY = ((0, 0, 0), (0, 1, 0), (0, 0, 1), (0, 1, 1), (0, 0, -1), (0, 1, -1), (-1, 1, 1), (1, 0, -1))
LATE = ((-2, 0, 1), (2, 1, -1), (0, 0, 2), (-1, 1, 2), (-2, 0, 2), (0, 1, -2), (1, 0, -2), (2, 1, -2))
B = 64
TERMS = 8
VMEM_LIMIT = 60 * 2**20
F32, BF16 = jnp.float32, jnp.bfloat16
NT = (((1,), (1,)), ((), ()))


def iota(shape, dim):
    return lax.broadcasted_iota(jnp.int32, shape, dim)


def order_kernel(t_ref, a_ref, b_ref):
    row, col = iota((256, 256), 0), iota((256, 256), 1)
    source = ((row >> 2) & 3) * 64 + (row >> 4) * 4 + (row & 3)
    pick = jnp.where(source == col, 1.0, 0.0).astype(BF16)
    for n in range(8):
        piece = t_ref[:, n * 256:(n + 1) * 256]
        turned = lax.dot_general(pick, piece, NT, preferred_element_type=F32).astype(BF16)
        a_ref[:, n] = turned[:, :128].reshape(16, 16, 128)
        b_ref[:, n] = turned[:, 128:].reshape(16, 16, 128)


def order_rows(block):
    half = jax.ShapeDtypeStruct((16, 16, 16, 128), BF16)
    spec = pl.BlockSpec((16, 8, 16, 128), lambda i: (0, i, 0, 0))
    return pl.pallas_call(
        order_kernel,
        grid=(2,),
        in_specs=[pl.BlockSpec((256, 2048), lambda i: (0, i))],
        out_specs=[spec, spec],
        out_shape=[half, half],
        compiler_params=pltpu.CompilerParams(vmem_limit_bytes=VMEM_LIMIT),
        cost_estimate=pl.CostEstimate(flops=2 * 16 * 256**3, bytes_accessed=2**22, transcendentals=0),
    )(block)


def choose_kernel(occ_list, virt_list, c_ref, o_ref):
    y, place = lax.axis_index("y"), lax.axis_index("x") * 2 + lax.axis_index("c")
    left = iota((B, 2 * B), 1) < B

    def one(n, carry):
        occ, virt = occ_list[y * 64 + n], virt_list[y * 64 + n]
        occ_here = (((occ >> 3) & 7) == place).astype(F32)
        virt_here = (((virt >> 3) & 7) == place).astype(F32)
        occ_block = c_ref[(occ >> 6) * 8 + (occ & 7)].astype(F32) * occ_here
        virt_block = c_ref[(virt >> 6) * 8 + (virt & 7)].astype(F32) * virt_here
        o_ref[n] = jnp.where(left, occ_block, virt_block).astype(BF16)
        return carry

    lax.fori_loop(0, 64, one, 0, unroll=8)


SMEM = pl.BlockSpec(memory_space=pltpu.SMEM)


def choose(held, occ_list, virt_list):
    return pl.pallas_call(
        choose_kernel,
        in_specs=[SMEM, SMEM, pl.BlockSpec(memory_space=pltpu.VMEM)],
        out_shape=jax.ShapeDtypeStruct((64, B, 2 * B), BF16),
        cost_estimate=pl.CostEstimate(flops=2**21, bytes_accessed=3 * 2**19, transcendentals=0),
    )(occ_list, virt_list, held)


def weight_kernel(count_ref, b_ref, w1_ref, w2_ref):
    pair = (lax.axis_index("y") * 4 + lax.axis_index("x")) * 2 + lax.axis_index("c")
    live = count_ref[pair]
    row, col = iota((256, 256), 0), iota((256, 256), 1)
    tall_row, tall_col = iota((256, B), 0), iota((256, B), 1)
    wide_row, wide_col = iota((B, 256), 0), iota((B, 256), 1)

    def one(hit):
        return jnp.where(hit, 1.0, 0.0).astype(BF16)

    left_virt = one((tall_row >> 4) * 4 + (tall_row & 3) == tall_col)
    right_virt = one((wide_col >> 4) * 4 + (wide_col & 3) == wide_row)
    keep_virt = ((row >> 2) & 3) == ((col >> 2) & 3)
    left_occ = one((tall_row >> 2) == tall_col)
    right_occ = one((wide_col >> 2) == wide_row)
    keep_occ = (row & 3) == (col & 3)
    for j in range(TERMS):
        both = b_ref[0, j].astype(F32)
        for n in range(1, 8):
            both += b_ref[n, j].astype(F32)
        both = jnp.where(j < live, both, 0.0).astype(BF16)
        occ, virt = both[:, :B], both[:, B:]
        spread = lax.dot_general(left_virt, virt, NT, preferred_element_type=F32).astype(BF16)
        spread = jnp.dot(spread, right_virt, preferred_element_type=F32)
        w1_ref[:, j] = jnp.where(keep_virt, spread, 0.0).astype(BF16).reshape(16, 16, 256)
        spread = lax.dot_general(left_occ, occ, NT, preferred_element_type=F32).astype(BF16)
        spread = jnp.dot(spread, right_occ, preferred_element_type=F32)
        w2_ref[:, j * 256:(j + 1) * 256] = jnp.where(keep_occ, spread, 0.0).astype(BF16)


def term_weights(term_count, blocks):
    return pl.pallas_call(
        weight_kernel,
        in_specs=[SMEM, pl.BlockSpec(memory_space=pltpu.VMEM)],
        out_shape=[
            jax.ShapeDtypeStruct((16, TERMS, 16, 256), BF16),
            jax.ShapeDtypeStruct((256, TERMS * 256), BF16),
        ],
        cost_estimate=pl.CostEstimate(flops=2**28, bytes_accessed=3 * 2**20, transcendentals=0),
    )(term_count, blocks)


def image_kernel(a_ref, b_ref, w1_ref, w2_ref, o_ref, half_ref):
    step = pl.program_id(0)

    @pl.when(step < 2)
    def _():
        for n in range(8):
            slab = jnp.concatenate([a_ref[:, n].reshape(256, 128), b_ref[:, n].reshape(256, 128)], axis=1)
            for g in range(0, 16, 2):
                part = w1_ref[g:g + 2].reshape(2 * TERMS * 16, 256)
                half = jnp.dot(part, slab, preferred_element_type=F32).astype(BF16)
                half_ref[g:g + 2, :, step * 8 + n] = half.reshape(2, TERMS, 16, 256)

    @pl.when(step >= 2)
    def _():
        for n in range(8):
            half = half_ref[(step - 2) * 8 + n].reshape(TERMS * 256, 256)
            image = jnp.dot(w2_ref[...], half, preferred_element_type=F32)
            o_ref[:, n * 256:(n + 1) * 256] = image.T.astype(BF16)


def image_rows(first, second, w1, w2):
    spec = pl.BlockSpec((16, 8, 16, 128), lambda i: (0, jnp.minimum(i, 1), 0, 0))
    return pl.pallas_call(
        image_kernel,
        grid=(4,),
        in_specs=[
            spec,
            spec,
            pl.BlockSpec((16, TERMS, 16, 256), lambda i: (0, 0, 0, 0)),
            pl.BlockSpec((256, TERMS * 256), lambda i: (0, 0)),
        ],
        out_specs=pl.BlockSpec((256, 2048), lambda i: (0, jnp.maximum(i - 2, 0))),
        out_shape=jax.ShapeDtypeStruct((256, 4096), BF16),
        scratch_shapes=[pltpu.VMEM((16, TERMS, 16, 16, 256), BF16)],
        compiler_params=pltpu.CompilerParams(vmem_limit_bytes=VMEM_LIMIT),
        cost_estimate=pl.CostEstimate(flops=2 * 256 * 256**3, bytes_accessed=6 * 2**20, transcendentals=0),
    )(first, second, w1, w2)


def tiles(images, columns, jobs, kind, base=None, given=()):
    count, width = len(images), len(columns)
    rows_of = [len(parts) * 128 for _, parts in jobs]

    def kernel(*refs):
        image_refs, column_refs = refs[:count], refs[count:count + width]
        sums = refs[len(refs) - len(jobs):]
        o_ref = refs[len(refs) - len(jobs) - 1]
        step = pl.program_id(0)
        for (held, parts), sum_ref in zip(jobs, sums):
            block = [column_refs[n][...].reshape(1024, 128) for n, _ in held]
            rows = [image_refs[i][h * 128:(h + 1) * 128] for i, h, _ in parts]
            part = jnp.dot(
                jnp.concatenate(rows, axis=0), jnp.concatenate(block, axis=1), preferred_element_type=F32
            )

            @pl.when(step == 0)
            def _():
                sum_ref[...] = part

            @pl.when(step > 0)
            def _():
                sum_ref[...] += part

        @pl.when(step == 3)
        def _():
            for (held, parts), sum_ref in zip(jobs, sums):
                for r, (_, _, place) in enumerate(parts):
                    for n, (_, side) in enumerate(held):
                        tile = sum_ref[r * 128:(r + 1) * 128, n * 128:(n + 1) * 128].T
                        o_ref[place // 2, 2 * side:2 * side + 2, place % 2] = tile.astype(kind).reshape(2, B, 128)
            for place, side in given:
                at = (place // 2, slice(2 * side, 2 * side + 2), place % 2)
                o_ref[at] = refs[count + width][at]

    whole = pl.BlockSpec((4, 4, 2, B, 128), lambda i: (0, 0, 0, 0, 0))
    flops = sum(2 * 4096 * r * 128 * len(held) for r, (held, _) in zip(rows_of, jobs))
    return pl.pallas_call(
        kernel,
        grid=(4,),
        in_specs=[pl.BlockSpec((256, 1024), lambda i: (0, i))] * count
        + [pl.BlockSpec((4, 16, 16, 128), lambda i: (i, 0, 0, 0))] * width
        + ([] if base is None else [whole]),
        out_specs=whole,
        out_shape=jax.ShapeDtypeStruct((4, 4, 2, B, 128), kind),
        scratch_shapes=[pltpu.VMEM((r, 128 * len(held)), F32) for r, (held, _) in zip(rows_of, jobs)],
        compiler_params=pltpu.CompilerParams(vmem_limit_bytes=VMEM_LIMIT),
        cost_estimate=pl.CostEstimate(
            flops=flops, bytes_accessed=(2 * count + width + 1) * 2**20, transcendentals=0
        ),
    )(*images, *columns, *([] if base is None else [base]))


ALL = ("y", "x", "c", "z")
ORB = ("y", "x", "c")
PLACES = [(y, x, c, z) for y in range(4) for x in range(4) for c in range(2) for z in range(8)]


def number(y, x, c, z):
    return ((y * 4 + x) * 2 + c) * 8 + z


def moved(value, target, places=PLACES):
    return lax.ppermute(value, ALL, [(number(*p), number(*target(*p))) for p in places])


def up(value):
    return moved(value, lambda y, x, c, z: (y, x, c, (z + 1) % 8))


def down(value):
    return moved(value, lambda y, x, c, z: (y, x, c, (z + 7) % 8))


def spread(block, axis, count):
    return lax.all_to_all(jnp.broadcast_to(block[None], (count,) + block.shape), axis, 0, 0)


def along_z(block):
    z = lax.axis_index("z")
    found = [block]
    for n in range(1, 8):
        found.append(moved(block, lambda y, x, c, z: (y, x, c, (z - n) % 8)))
    return jnp.roll(jnp.stack(found), z, axis=0)


def add_up(pieces):
    arrived = lax.all_to_all(pieces.reshape(32, B, 128), ORB, 0, 0)
    return arrived.astype(F32).sum(0) * (0.25 / B)


def placed(total, group):
    def target(y, x, c, z):
        row, _, col = group[y * 2 + c]
        orb = ((z + col) % 8) * 4 + x
        return orb // 8, orb // 2 % 4, orb % 2, (z + row) % 8

    halves = [[p for p in PLACES if group[p[0] * 2 + p[2]][1] == half] for half in range(2)]
    return [moved(total, target, places) for places in halves]


def body(three_centre, occ_blocks, virt_blocks, occ_list, virt_list, term_count):
    both = jnp.concatenate([occ_blocks[0], virt_blocks[0]], axis=1)
    own = order_rows(three_centre[0])
    column = along_z(both)
    own, column = lax.optimization_barrier((own, column))
    below_first, above_first = up(own[0]), down(own[1])
    below_last, above_last = up(own[1]), down(own[0])
    far_below_first, far_above_first = up(below_first), down(above_first)

    held = spread(column, "y", 4).reshape(32, B, 2 * B)
    chosen = choose(held, occ_list, virt_list)
    arrived = lax.all_to_all(chosen.reshape(8, 8, B, 2 * B), ("x", "c"), 0, 0)
    w1, w2 = term_weights(term_count, arrived)
    image = image_rows(own[0], own[1], w1, w2)

    image, below_last, above_last = lax.optimization_barrier((image, below_last, above_last))
    far_below_last, far_above_last = up(below_last), down(above_last)
    near = image_rows(below_last, above_last, w1, w2)
    early = tiles(
        [image, near],
        [own[0], own[1], above_last, above_first, below_first, below_last],
        [
            ([(0, 0), (1, 1)], [(0, 0, 0), (0, 1, 1)]),
            ([(2, 0), (3, 1)], [(0, 0, 2), (0, 1, 3), (1, 0, 6)]),
            ([(4, 0), (5, 1)], [(0, 0, 4), (0, 1, 5), (1, 1, 7)]),
        ],
        F32,
    )
    early, far_below_first, far_above_first = lax.optimization_barrier((early, far_below_first, far_above_first))
    early = add_up(early)
    far = image_rows(far_below_first, far_above_first, w1, w2)
    late_above = [(0, 0, 2), (1, 0, 3), (2, 0, 4)]
    late_below = [(0, 1, 5), (1, 1, 6), (2, 1, 7)]
    late = tiles(
        [image, near, far],
        [above_last, above_first, below_first, below_last, far_above_first, far_below_first],
        [
            ([(0, 0), (1, 1)], [(2, 0, 0)]),
            ([(2, 0), (3, 1)], [(2, 1, 1)]),
            ([(4, 1)], late_above),
            ([(5, 0)], late_below),
        ],
        BF16,
    )
    late, early, far_above_last, far_below_last = lax.optimization_barrier(
        (late, early, far_above_last, far_below_last)
    )
    early = placed(early, EARLY)
    late = tiles(
        [image, near, far],
        [far_above_last, far_below_last],
        [([(0, 0)], late_above), ([(1, 1)], late_below)],
        BF16,
        late,
        [(0, 0), (0, 1), (1, 0), (1, 1), (2, 1), (3, 1), (4, 1), (5, 0), (6, 0), (7, 0)],
    )
    late = placed(add_up(late), LATE)
    return jnp.concatenate([e + l for e, l in zip(early, late)], axis=1).T


def solution(mesh):
    fine = Mesh(mesh.devices.reshape(4, 4, 2, 8), ALL)
    blocks = P(ALL, None, None)
    inputs = (P(ORB, "z", None), blocks, blocks, P(), P(), P())
    return jax.shard_map(body, mesh=fine, in_specs=inputs, out_specs=P("z", ORB), check_vma=False)
```

time: 561 us -> 183 us (0.33)
  waiting for transfers between devices: 468 us -> 35.8 us
  Pallas kernels: 0 us -> 75.1 us
  starting transfers between devices: 0.12 us -> 62.8 us
  matrix products: 28.3 us -> 0 us
  local copies, waits for them, and re-layouts: 28.2 us -> 3.93 us
  between operations: 13.2 us -> 0.18 us
  other arithmetic: 11.2 us -> 1.63 us
  loops' own time: 9.42 us -> 0 us
    all_gather x3 -> x0, waiting for transfers between devices: 345 us -> none  [the longest x1 118 us: body(): lax.all_gather(local_block, 'aux', axis=0, tiled=True)]
    reduce_scatter x1 -> x0, waiting for transfers between devices: 120 us -> none  [body(): lax.psum_scatter(partial_sums, 'orb', scatter_dimension=1, tiled=True)]
    pallas_call x0 -> x9, Pallas kernels: none -> 75.1 us  [the longest x3 37.9 us: image_rows(): pl.pallas_call(image_kernel, grid=(4,), in_specs=[spec, spec, pl.BlockSpe...]
    ppermute x0 -> x19, starting transfers between devices: none -> 38.3 us  [moved(): lax.ppermute(value, ALL, [(number(*p), number(*target(*p))) for p in plac...]
    ppermute x0 -> x19, waiting for transfers between devices: none -> 29.6 us  [moved(): lax.ppermute(value, ALL, [(number(*p), number(*target(*p))) for p in plac...]
    dot_general x5 -> x0, matrix products: 28.3 us -> none  [the longest x1 13 us: body(): lax.dot_general(image_rows, lax.all_gather(local_block, 'aux', axis=0, ti...]
    all_to_all x0 -> x4, starting transfers between devices: none -> 24.5 us  [the longest x2 14.9 us: add_up(): arrived = lax.all_to_all(pieces.reshape(32, B, 128), ORB, 0, 0)]
    reshape x2 -> x0, local copies, waits for them, and re-layouts: 11.1 us -> none  [term_value(): half_image.astype(jnp.bfloat16).reshape(aux_rows, block_width, block_width)]
  transfers between devices with their start and end apart: 4 -> 23, of which waited for: 4 -> 10; matrix products, arithmetic and copies ran while one was open for 10% -> 0% of each run, Pallas kernels for 0% -> 37%
where the time goes in v2:
time: 183 us; the launch traced here: 179 us
  Pallas kernels  75.1 us (41%)
  starting transfers between devices  62.8 us (34%)
  waiting for transfers between devices  35.8 us (20%)
  local copies, waits for them, and re-layouts  3.93 us (2%)
    ppermute x19, starting transfers between devices, moved(): lax.ppermute(value, ALL, [(number(*p), number(*target(*p))) for p in plac...  38.3 us
    pallas_call x3, Pallas kernels, image_rows(): pl.pallas_call(image_kernel, grid=(4,), in_specs=[spec, spec, pl.BlockSpe...  37.9 us
    ppermute x19, waiting for transfers between devices, moved(): lax.ppermute(value, ALL, [(number(*p), number(*target(*p))) for p in plac...  29.6 us
    pallas_call x3, Pallas kernels, tiles(): pl.pallas_call(kernel, grid=(4,), in_specs=[pl.BlockSpec((256, 1024), lam...  26.9 us
    all_to_all x2, starting transfers between devices, add_up(): arrived = lax.all_to_all(pieces.reshape(32, B, 128), ORB, 0, 0)  14.9 us
    all_to_all x1, starting transfers between devices, body(): arrived = lax.all_to_all(chosen.reshape(8, 8, B, 2 * B), ('x', 'c'), 0, 0)  4.8 us
    all_to_all x1, starting transfers between devices, spread(): lax.all_to_all(jnp.broadcast_to(block[None], (count,) + block.shape), axi...  4.8 us
    pallas_call x1, Pallas kernels, term_weights(): pl.pallas_call(weight_kernel, in_specs=[SMEM, pl.BlockSpec(memory_space=p...  4.38 us
  transfers between devices with their start and end apart: 23, of which 10 were waited for; matrix products, arithmetic and copies ran while one was open for 0% of the time, Pallas kernels for 37%

profile of v2, /device:TPU:20, one launch (start us, length us, event | category | flops | bytes accessed | tf_op | source)
XLA Modules:
  0.0 179.4 jit_solution(2534289956934978466)
XLA Ops:
  0.8 5.9 %collective-permute-start = (bf16[64,128]{1,0:T(8,128)(2,1)S(1)}, bf16[64,128]{1,0:T(8,128)(2,1)S(1)}, u32[]{:S(2)}, u32[]{:S(2)}) collective-permute-start(bf16[64,128]{1,0:T(8,128)(2,1)S(1)} %get-tuple-element.40), channel_id=1, source_target_pairs={{0,7},{1,0},{2,1},{3,2},{4,3},{5,4},{6,5},{7,6},{8,15},{9,8},{10,9... | collective-permute-start | bytes 49160 | tf_op jit(solution)/shard_map/ppermute | solution.py:218
  6.7 1.5 collective-permute-start.1
  8.6 5.0 %collective-permute-start.3 = (bf16[64,128]{1,0:T(8,128)(2,1)S(1)}, bf16[64,128]{1,0:T(8,128)(2,1)S(1)}, u32[]{:S(2)}, u32[]{:S(2)}) collective-permute-start(bf16[64,128]{1,0:T(8,128)(2,1)S(1)} %get-tuple-element.40), channel_id=1, source_target_pairs={{0,4},{1,5},{2,6},{3,7},{4,0},{5,1},{6,2},{7,3},{8,12},{9,13},{10,... | collective-permute-start | bytes 49160 | tf_op jit(solution)/shard_map/ppermute | solution.py:218
  13.7 3.3 %shard_map.64 = (bf16[16,16,16,128]{3,2,1,0:T(8,128)(2,1)}, bf16[16,16,16,128]{3,2,1,0:T(8,128)(2,1)}) custom-call(bf16[256,4096]{1,0:T(8,128)(2,1)} %bitcast.36), custom_call_target="tpu_custom_call" | custom-call | flops 536870912 | bytes 4194304 | tf_op jit(solution)/shard_map/pallas_call | solution.py:35
  16.9 2.5 %collective-permute-start.5 = (bf16[64,128]{1,0:T(8,128)(2,1)S(1)}, bf16[64,128]{1,0:T(8,128)(2,1)S(1)}, u32[]{:S(2)}, u32[]{:S(2)}) collective-permute-start(bf16[64,128]{1,0:T(8,128)(2,1)S(1)} %get-tuple-element.40), channel_id=1, source_target_pairs={{0,2},{1,3},{2,4},{3,5},{4,6},{5,7},{6,0},{7,1},{8,10},{9,11},{10,... | collective-permute-start | bytes 49160 | tf_op jit(solution)/shard_map/ppermute | solution.py:218
  19.4 1.9 %collective-permute-start.6 = (bf16[64,128]{1,0:T(8,128)(2,1)S(1)}, bf16[64,128]{1,0:T(8,128)(2,1)S(1)}, u32[]{:S(2)}, u32[]{:S(2)}) collective-permute-start(bf16[64,128]{1,0:T(8,128)(2,1)S(1)} %get-tuple-element.40), channel_id=1, source_target_pairs={{0,1},{1,2},{2,3},{3,4},{4,5},{5,6},{6,7},{7,0},{8,9},{9,10},{10,1... | collective-permute-start | bytes 49160 | tf_op jit(solution)/shard_map/ppermute | solution.py:218
  21.4 1.9 %collective-permute-done.5 = bf16[64,128]{1,0:T(8,128)(2,1)S(1)} collective-permute-done((bf16[64,128]{1,0:T(8,128)(2,1)S(1)}, bf16[64,128]{1,0:T(8,128)(2,1)S(1)}, u32[]{:S(2)}, u32[]{:S(2)}) %collective-permute-start.5) | collective-permute-done | bytes 16416 | tf_op jit(solution)/shard_map/ppermute | solution.py:218
  25.4 4.8 %all-to-all-start = ((bf16[4,8,64,128]{3,2,1,0:T(8,128)(2,1)}), bf16[4,8,64,128]{3,2,1,0:T(8,128)(2,1)S(1)}, u32[]{:S(2)}, u32[]{:S(2)}) async-start(bf16[4,8,64,128]{3,2,1,0:T(8,128)(2,1)} %broadcast_in_dim.2), calls=%async_computation | async-start | bytes 1048576 | tf_op jit(solution)/shard_map/all_to_all | solution.py:230
  30.9 2.5 %collective-permute-start.9 = (bf16[16,16,16,128]{3,2,1,0:T(8,128)(2,1)}, bf16[16,16,16,128]{3,2,1,0:T(8,128)(2,1)}, u32[]{:S(2)}, u32[]{:S(2)}) collective-permute-start(bf16[16,16,16,128]{3,2,1,0:T(8,128)(2,1)} %get-tuple-element.25.b_ref.refs_3_), channel_id=1, source_target_pairs={{0,7},{1,0},{2,1},{3,2},{4,3},{5,4},{6,5},{7,6},{8,15},{9,8},{10,9... | collective-permute-start | bytes 3145736 | tf_op jit(solution)/shard_map/ppermute | solution.py:218
  33.5 1.9 %all-to-all-done = bf16[4,8,64,128]{3,2,1,0:T(8,128)(2,1)S(1)} async-done(((bf16[4,8,64,128]{3,2,1,0:T(8,128)(2,1)}), bf16[4,8,64,128]{3,2,1,0:T(8,128)(2,1)S(1)}, u32[]{:S(2)}, u32[]{:S(2)}) %all-to-all-start) | async-done | bytes 524320 | tf_op jit(solution)/shard_map/all_to_all | solution.py:230
  36.2 2.6 %shard_map.65 = bf16[64,64,128]{2,1,0:T(8,128)(2,1)} custom-call(s32[256]{0:T(256)} %occ_list.1, s32[256]{0:T(256)} %virt_list.1, bf16[32,64,128]{2,1,0:T(8,128)(2,1)} %bitcast.37), custom_call_target="tpu_custom_call" | custom-call | flops 2097152 | bytes 1572864 | tf_op jit(solution)/shard_map/pallas_call | solution.py:66
  38.8 4.8 %all-to-all-start.1 = ((bf16[8,8,64,128]{3,2,1,0:T(8,128)(2,1)}), bf16[8,8,64,128]{3,2,1,0:T(8,128)(2,1)S(1)}, u32[]{:S(2)}, u32[]{:S(2)}) async-start(bf16[8,8,64,128]{3,2,1,0:T(8,128)(2,1)} %bitcast.33), calls=%async_computation.1 | async-start | bytes 2097152 | tf_op jit(solution)/shard_map/all_to_all | solution.py:267
  44.3 2.5 %collective-permute-start.8 = (bf16[16,16,16,128]{3,2,1,0:T(8,128)(2,1)}, bf16[16,16,16,128]{3,2,1,0:T(8,128)(2,1)}, u32[]{:S(2)}, u32[]{:S(2)}) collective-permute-start(bf16[16,16,16,128]{3,2,1,0:T(8,128)(2,1)} %get-tuple-element.24.a_ref.refs_2_), channel_id=1, source_target_pairs={{0,7},{1,0},{2,1},{3,2},{4,3},{5,4},{6,5},{7,6},{8,15},{9,8},{10,9... | collective-permute-start | bytes 3145736 | tf_op jit(solution)/shard_map/ppermute | solution.py:218
  46.8 10.9 %collective-permute-done.10.refs_6_.refs_5_ = bf16[16,16,16,128]{3,2,1,0:T(8,128)(2,1)S(1)} collective-permute-done((bf16[16,16,16,128]{3,2,1,0:T(8,128)(2,1)}, bf16[16,16,16,128]{3,2,1,0:T(8,128)(2,1)S(1)}, u32[]{:S(2)}, u32[]{:S(2)}) %collective-permute-start.10) | collective-permute-done | bytes 1048608 | tf_op jit(solution)/shard_map/ppermute | solution.py:218
  57.8 3.3 %collective-permute-start.12 = (bf16[16,16,16,128]{3,2,1,0:T(8,128)(2,1)}, bf16[16,16,16,128]{3,2,1,0:T(8,128)(2,1)}, u32[]{:S(2)}, u32[]{:S(2)}) collective-permute-start(bf16[16,16,16,128]{3,2,1,0:T(8,128)(2,1)} %collective-permute-done.9.refs_5_.refs_4_), channel_id=1, source_target_pairs={{0,7},{1,0},{2,1},{3,2},{4,3},{5,4},{6,5},{7,6},{8,15},{9,8},{10,9... | collective-permute-start | bytes 3145736 | tf_op jit(solution)/shard_map/ppermute | solution.py:218
  62.1 4.4 %shard_map.66 = (bf16[16,8,16,256]{3,2,1,0:T(8,128)(2,1)}, bf16[256,2048]{1,0:T(8,128)(2,1)}) custom-call(s32[32]{0:T(128)} %count_ref.1, bf16[8,8,64,128]{3,2,1,0:T(8,128)(2,1)} %copy-done), custom_call_target="tpu_custom_call" | custom-call | flops 268435456 | bytes 3145728 | tf_op jit(solution)/shard_map/pallas_call | solution.py:105
  66.5 12.6 %shard_map.67.refs_0_ = bf16[256,4096]{1,0:T(8,128)(2,1)} custom-call(bf16[16,16,16,128]{3,2,1,0:T(8,128)(2,1)} %get-tuple-element.24.a_ref.refs_2_, bf16[16,16,16,128]{3,2,1,0:T(8,128)(2,1)} %get-tuple-element.25.b_ref.refs_3_, bf16[16,8,16,256]{3,2,1,0:T(8,128)(2,1)} %get-tuple-element.27.w1_ref, bf16[256,2048]{1,0:T(8,128)(2,1)} %get-tuple-element.28.w2_ref), custom_call_target="tpu_custom_call" | custom-call | flops 8589934592 | bytes 6291456 | tf_op jit(solution)/shard_map/pallas_call | solution.py:138
  81.2 12.6 %shard_map.68.refs_1_ = bf16[256,4096]{1,0:T(8,128)(2,1)} custom-call(bf16[16,16,16,128]{3,2,1,0:T(8,128)(2,1)} %copy-done.2, bf16[16,16,16,128]{3,2,1,0:T(8,128)(2,1)} %collective-permute-done.8.b_ref.refs_4_.refs_3_, bf16[16,8,16,256]{3,2,1,0:T(8,128)(2,1)} %get-tuple-element.27.w1_ref, bf16[256,2048]{1,0:T(8,128)(2,1)} %get-tuple-element.28.w2_ref), custom_call_target="tpu_custom_call" | custom-call | flops 8589934592 | bytes 6291456 | tf_op jit(solution)/shard_map/pallas_call | solution.py:138
  93.8 9.2 %shard_map.69 = f32[4,4,2,64,128]{4,3,2,1,0:T(8,128)} custom-call(bf16[256,4096]{1,0:T(8,128)(2,1)} %shard_map.67.refs_0_, bf16[256,4096]{1,0:T(8,128)(2,1)} %shard_map.68.refs_1_, bf16[16,16,16,128]{3,2,1,0:T(8,128)(2,1)} %get-tuple-element.24.a_ref.refs_2_, bf16[16,16,16,128]{3,2,1,0:T(8,128)(2,1)} %get-tuple-element.25.b_ref.refs_3_, ...), custom_call_target="tpu_custom_call" | custom-call | flops 2147483648 | bytes 11534336 | tf_op jit(solution)/shard_map/pallas_call | solution.py:192
  103.0 7.5 %all-to-all-start.2 = ((f32[32,64,128]{2,1,0:T(8,128)}), f32[32,64,128]{2,1,0:T(8,128)S(1)}, u32[]{:S(2)}, u32[]{:S(2)}) async-start(f32[32,64,128]{2,1,0:T(8,128)} %bitcast.34), calls=%async_computation.2 | async-start | bytes 2097152 | tf_op jit(solution)/shard_map/all_to_all | solution.py:242
  110.5 2.6 %collective-permute-start.13 = (bf16[16,16,16,128]{3,2,1,0:T(8,128)(2,1)}, bf16[16,16,16,128]{3,2,1,0:T(8,128)(2,1)S(1)}, u32[]{:S(2)}, u32[]{:S(2)}) collective-permute-start(bf16[16,16,16,128]{3,2,1,0:T(8,128)(2,1)} %collective-permute-done.8.b_ref.refs_4_.refs_3_), channel_id=1, source_target_pairs={{0,7},{1,0},{2,1},{3,2},{4,3},{5,4},{6,5},{7,6},{8,15},{9,8},{10,9... | collective-permute-start | bytes 3145736 | tf_op jit(solution)/shard_map/ppermute | solution.py:218
  113.2 12.7 %shard_map.70.refs_2_ = bf16[256,4096]{1,0:T(8,128)(2,1)} custom-call(bf16[16,16,16,128]{3,2,1,0:T(8,128)(2,1)} %collective-permute-done.11.a_ref.refs_8_, bf16[16,16,16,128]{3,2,1,0:T(8,128)(2,1)} %collective-permute-done.12.b_ref.refs_7_, bf16[16,8,16,256]{3,2,1,0:T(8,128)(2,1)} %get-tuple-element.27.w1_ref, bf16[256,2048]{1,0:T(8,128)(2,1)} %get-tuple-element.28.w2_ref), custom_call_target="tpu_custom_call" | custom-call | flops 8589934592 | bytes 6291456 | tf_op jit(solution)/shard_map/pallas_call | solution.py:138
  125.9 9.8 %shard_map.71.refs_5_ = bf16[4,4,2,64,128]{4,3,2,1,0:T(8,128)(2,1)} custom-call(bf16[256,4096]{1,0:T(8,128)(2,1)} %shard_map.67.refs_0_, bf16[256,4096]{1,0:T(8,128)(2,1)} %shard_map.68.refs_1_, bf16[256,4096]{1,0:T(8,128)(2,1)} %shard_map.70.refs_2_, bf16[16,16,16,128]{3,2,1,0:T(8,128)(2,1)} %collective-permute-done.8.b_ref.refs_4_.refs_3_, ...), custom_call_target="tpu_custom_call" | custom-call | flops 1342177280 | bytes 13631488 | tf_op jit(solution)/shard_map/pallas_call | solution.py:192
  136.3 3.2 %collective-permute-done.14.refs_4_ = bf16[16,16,16,128]{3,2,1,0:T(8,128)(2,1)} collective-permute-done((bf16[16,16,16,128]{3,2,1,0:T(8,128)(2,1)S(1)}, bf16[16,16,16,128]{3,2,1,0:T(8,128)(2,1)}, u32[]{:S(2)}, u32[]{:S(2)}) %collective-permute-start.14) | collective-permute-done | bytes 1048608 | tf_op jit(solution)/shard_map/ppermute | solution.py:218
  139.4 7.9 %shard_map.72 = bf16[4,4,2,64,128]{4,3,2,1,0:T(8,128)(2,1)} custom-call(bf16[256,4096]{1,0:T(8,128)(2,1)} %shard_map.67.refs_0_, bf16[256,4096]{1,0:T(8,128)(2,1)} %shard_map.68.refs_1_, bf16[256,4096]{1,0:T(8,128)(2,1)} %shard_map.70.refs_2_, bf16[16,16,16,128]{3,2,1,0:T(8,128)(2,1)} %copy-done.5, ...), custom_call_target="tpu_custom_call" | custom-call | flops 805306368 | bytes 9437184 | tf_op jit(solution)/shard_map/pallas_call | solution.py:192
  147.4 7.4 %all-to-all-start.3 = ((bf16[32,64,128]{2,1,0:T(8,128)(2,1)}), bf16[32,64,128]{2,1,0:T(8,128)(2,1)S(1)}, u32[]{:S(2)}, u32[]{:S(2)}) async-start(bf16[32,64,128]{2,1,0:T(8,128)(2,1)} %bitcast.35), calls=%async_computation.3 | async-start | bytes 1048576 | tf_op jit(solution)/shard_map/all_to_all | solution.py:242
  154.8 3.7 %collective-permute-start.15 = (f32[64,128]{1,0:T(8,128)S(1)}, f32[64,128]{1,0:T(8,128)S(1)}, u32[]{:S(2)}, u32[]{:S(2)}) collective-permute-start(f32[64,128]{1,0:T(8,128)S(1)} %broadcast_multiply_fusion.1), channel_id=1, source_target_pairs={{0,0},{1,33},{2,66},{3,99},{4,132},{5,165},{6,198},{7,231},{16,8},... | collective-permute-start | bytes 98312 | tf_op jit(solution)/shard_map/ppermute | solution.py:218
  158.5 4.3 %all-to-all-done.3 = bf16[32,64,128]{2,1,0:T(8,128)(2,1)S(1)} async-done(((bf16[32,64,128]{2,1,0:T(8,128)(2,1)}), bf16[32,64,128]{2,1,0:T(8,128)(2,1)S(1)}, u32[]{:S(2)}, u32[]{:S(2)}) %all-to-all-start.3) | async-done | bytes 524320 | tf_op jit(solution)/shard_map/all_to_all | solution.py:242
  162.9 2.9 %collective-permute-start.16 = (f32[64,128]{1,0:T(8,128)S(1)}, f32[64,128]{1,0:T(8,128)S(1)}, u32[]{:S(2)}, u32[]{:S(2)}) collective-permute-start(f32[64,128]{1,0:T(8,128)S(1)} %broadcast_multiply_fusion), channel_id=1, source_target_pairs={{0,38},{1,71},{2,96},{3,129},{4,162},{5,195},{6,228},{7,5},{16,46}... | collective-permute-start | bytes 98312 | tf_op jit(solution)/shard_map/ppermute | solution.py:218
  166.5 1.3 collective-permute-start.18
  167.8 5.4 %collective-permute-done.16 = f32[64,128]{1,0:T(8,128)S(1)} collective-permute-done((f32[64,128]{1,0:T(8,128)S(1)}, f32[64,128]{1,0:T(8,128)S(1)}, u32[]{:S(2)}, u32[]{:S(2)}) %collective-permute-start.16) | collective-permute-done | bytes 32800 | tf_op jit(solution)/shard_map/ppermute | solution.py:218
  173.2 5.5 %collective-permute-done.18 = f32[64,128]{1,0:T(8,128)S(1)} collective-permute-done((f32[64,128]{1,0:T(8,128)S(1)}, f32[64,128]{1,0:T(8,128)S(1)}, u32[]{:S(2)}, u32[]{:S(2)}) %collective-permute-start.18) | collective-permute-done | bytes 32800 | tf_op jit(solution)/shard_map/ppermute | solution.py:218
  (60 shorter events, 10.8 us)
Async XLA Ops:
  0.8 16.1 %collective-permute-start = (bf16[64,128]{1,0:T(8,128)(2,1)S(1)}, bf16[64,128]{1,0:T(8,128)(2,1)S(1)}, u32[]{:S(2)}, u32[]{:S(2)}) collective-permute-start(bf16[64,128]{1,0:T(8,128)(2,1)S(1)} %get-tuple-element.40), channel_id=1, source_target_pairs={{0,7},{1,0},{2,1},{3,2},{4,3},{5,4},{6,5},{7,6},{8,15},{9,8},{10,9... | collective-permute-start | bytes 49160 | tf_op jit(solution)/shard_map/ppermute | solution.py:218
  6.7 12.7 %collective-permute-start.1 = (bf16[64,128]{1,0:T(8,128)(2,1)S(1)}, bf16[64,128]{1,0:T(8,128)(2,1)S(1)}, u32[]{:S(2)}, u32[]{:S(2)}) collective-permute-start(bf16[64,128]{1,0:T(8,128)(2,1)S(1)} %get-tuple-element.40), channel_id=1, source_target_pairs={{0,6},{1,7},{2,0},{3,1},{4,2},{5,3},{6,4},{7,5},{8,14},{9,15},{10,... | collective-permute-start | bytes 49160 | tf_op jit(solution)/shard_map/ppermute | solution.py:218
  8.2 13.2 %collective-permute-start.2 = (bf16[64,128]{1,0:T(8,128)(2,1)S(1)}, bf16[64,128]{1,0:T(8,128)(2,1)S(1)}, u32[]{:S(2)}, u32[]{:S(2)}) collective-permute-start(bf16[64,128]{1,0:T(8,128)(2,1)S(1)} %get-tuple-element.40), channel_id=1, source_target_pairs={{0,5},{1,6},{2,7},{3,0},{4,1},{5,2},{6,3},{7,4},{8,13},{9,14},{10,... | collective-permute-start | bytes 49160 | tf_op jit(solution)/shard_map/ppermute | solution.py:218
  8.6 12.7 %collective-permute-start.3 = (bf16[64,128]{1,0:T(8,128)(2,1)S(1)}, bf16[64,128]{1,0:T(8,128)(2,1)S(1)}, u32[]{:S(2)}, u32[]{:S(2)}) collective-permute-start(bf16[64,128]{1,0:T(8,128)(2,1)S(1)} %get-tuple-element.40), channel_id=1, source_target_pairs={{0,4},{1,5},{2,6},{3,7},{4,0},{5,1},{6,2},{7,3},{8,12},{9,13},{10,... | collective-permute-start | bytes 49160 | tf_op jit(solution)/shard_map/ppermute | solution.py:218
  13.7 7.7 %collective-permute-start.4 = (bf16[64,128]{1,0:T(8,128)(2,1)S(1)}, bf16[64,128]{1,0:T(8,128)(2,1)S(1)}, u32[]{:S(2)}, u32[]{:S(2)}) collective-permute-start(bf16[64,128]{1,0:T(8,128)(2,1)S(1)} %get-tuple-element.40), channel_id=1, source_target_pairs={{0,3},{1,4},{2,5},{3,6},{4,7},{5,0},{6,1},{7,2},{8,11},{9,12},{10,... | collective-permute-start | bytes 49160 | tf_op jit(solution)/shard_map/ppermute | solution.py:218
  16.9 6.3 %collective-permute-start.5 = (bf16[64,128]{1,0:T(8,128)(2,1)S(1)}, bf16[64,128]{1,0:T(8,128)(2,1)S(1)}, u32[]{:S(2)}, u32[]{:S(2)}) collective-permute-start(bf16[64,128]{1,0:T(8,128)(2,1)S(1)} %get-tuple-element.40), channel_id=1, source_target_pairs={{0,2},{1,3},{2,4},{3,5},{4,6},{5,7},{6,0},{7,1},{8,10},{9,11},{10,... | collective-permute-start | bytes 49160 | tf_op jit(solution)/shard_map/ppermute | solution.py:218
  19.4 5.0 %collective-permute-start.6 = (bf16[64,128]{1,0:T(8,128)(2,1)S(1)}, bf16[64,128]{1,0:T(8,128)(2,1)S(1)}, u32[]{:S(2)}, u32[]{:S(2)}) collective-permute-start(bf16[64,128]{1,0:T(8,128)(2,1)S(1)} %get-tuple-element.40), channel_id=1, source_target_pairs={{0,1},{1,2},{2,3},{3,4},{4,5},{5,6},{6,7},{7,0},{8,9},{9,10},{10,1... | collective-permute-start | bytes 49160 | tf_op jit(solution)/shard_map/ppermute | solution.py:218
  25.4 9.9 %all-to-all-start = ((bf16[4,8,64,128]{3,2,1,0:T(8,128)(2,1)}), bf16[4,8,64,128]{3,2,1,0:T(8,128)(2,1)S(1)}, u32[]{:S(2)}, u32[]{:S(2)}) async-start(bf16[4,8,64,128]{3,2,1,0:T(8,128)(2,1)} %broadcast_in_dim.2), calls=%async_computation | async-start | bytes 1048576 | tf_op jit(solution)/shard_map/all_to_all | solution.py:230
  30.2 27.5 %collective-permute-start.10 = (bf16[16,16,16,128]{3,2,1,0:T(8,128)(2,1)}, bf16[16,16,16,128]{3,2,1,0:T(8,128)(2,1)S(1)}, u32[]{:S(2)}, u32[]{:S(2)}) collective-permute-start(bf16[16,16,16,128]{3,2,1,0:T(8,128)(2,1)} %get-tuple-element.24.a_ref.refs_2_), channel_id=1, source_target_pairs={{0,1},{1,2},{2,3},{3,4},{4,5},{5,6},{6,7},{7,0},{8,9},{9,10},{10,1... | collective-permute-start | bytes 3145736 | tf_op jit(solution)/shard_map/ppermute | solution.py:218
  30.9 26.8 %collective-permute-start.9 = (bf16[16,16,16,128]{3,2,1,0:T(8,128)(2,1)}, bf16[16,16,16,128]{3,2,1,0:T(8,128)(2,1)}, u32[]{:S(2)}, u32[]{:S(2)}) collective-permute-start(bf16[16,16,16,128]{3,2,1,0:T(8,128)(2,1)} %get-tuple-element.25.b_ref.refs_3_), channel_id=1, source_target_pairs={{0,7},{1,0},{2,1},{3,2},{4,3},{5,4},{6,5},{7,6},{8,15},{9,8},{10,9... | collective-permute-start | bytes 3145736 | tf_op jit(solution)/shard_map/ppermute | solution.py:218
  35.3 0.8 copy-start.4
  38.8 22.3 %all-to-all-start.1 = ((bf16[8,8,64,128]{3,2,1,0:T(8,128)(2,1)}), bf16[8,8,64,128]{3,2,1,0:T(8,128)(2,1)S(1)}, u32[]{:S(2)}, u32[]{:S(2)}) async-start(bf16[8,8,64,128]{3,2,1,0:T(8,128)(2,1)} %bitcast.33), calls=%async_computation.1 | async-start | bytes 2097152 | tf_op jit(solution)/shard_map/all_to_all | solution.py:267
  43.6 36.6 %collective-permute-start.7 = (bf16[16,16,16,128]{3,2,1,0:T(8,128)(2,1)}, bf16[16,16,16,128]{3,2,1,0:T(8,128)(2,1)S(1)}, u32[]{:S(2)}, u32[]{:S(2)}) collective-permute-start(bf16[16,16,16,128]{3,2,1,0:T(8,128)(2,1)} %get-tuple-element.25.b_ref.refs_3_), channel_id=1, source_target_pairs={{0,1},{1,2},{2,3},{3,4},{4,5},{5,6},{6,7},{7,0},{8,9},{9,10},{10,1... | collective-permute-start | bytes 3145736 | tf_op jit(solution)/shard_map/ppermute | solution.py:218
  44.3 35.9 %collective-permute-start.8 = (bf16[16,16,16,128]{3,2,1,0:T(8,128)(2,1)}, bf16[16,16,16,128]{3,2,1,0:T(8,128)(2,1)}, u32[]{:S(2)}, u32[]{:S(2)}) collective-permute-start(bf16[16,16,16,128]{3,2,1,0:T(8,128)(2,1)} %get-tuple-element.24.a_ref.refs_2_), channel_id=1, source_target_pairs={{0,7},{1,0},{2,1},{3,2},{4,3},{5,4},{6,5},{7,6},{8,15},{9,8},{10,9... | collective-permute-start | bytes 3145736 | tf_op jit(solution)/shard_map/ppermute | solution.py:218
  57.7 21.4 %copy-start.1 = (bf16[16,16,16,128]{3,2,1,0:T(8,128)(2,1)}, bf16[16,16,16,128]{3,2,1,0:T(8,128)(2,1)S(1)}, u32[]{:S(2)}) copy-start(bf16[16,16,16,128]{3,2,1,0:T(8,128)(2,1)S(1)} %collective-permute-done.10.refs_6_.refs_5_) | copy-start | bytes 3145732
  57.7 45.3 %collective-permute-start.11 = (bf16[16,16,16,128]{3,2,1,0:T(8,128)(2,1)S(1)}, bf16[16,16,16,128]{3,2,1,0:T(8,128)(2,1)}, u32[]{:S(2)}, u32[]{:S(2)}) collective-permute-start(bf16[16,16,16,128]{3,2,1,0:T(8,128)(2,1)S(1)} %collective-permute-done.10.refs_6_.refs_5_), channel_id=1, source_target_pairs={{0,1},{1,2},{2,3},{3,4},{4,5},{5,6},{6,7},{7,0},{8,9},{9,10},{10,1... | collective-permute-start | bytes 3145736 | tf_op jit(solution)/shard_map/ppermute | solution.py:218
  57.8 45.3 %collective-permute-start.12 = (bf16[16,16,16,128]{3,2,1,0:T(8,128)(2,1)}, bf16[16,16,16,128]{3,2,1,0:T(8,128)(2,1)}, u32[]{:S(2)}, u32[]{:S(2)}) collective-permute-start(bf16[16,16,16,128]{3,2,1,0:T(8,128)(2,1)} %collective-permute-done.9.refs_5_.refs_4_), channel_id=1, source_target_pairs={{0,7},{1,0},{2,1},{3,2},{4,3},{5,4},{6,5},{7,6},{8,15},{9,8},{10,9... | collective-permute-start | bytes 3145736 | tf_op jit(solution)/shard_map/ppermute | solution.py:218
  61.1 1.0 copy-start
  80.2 1.0 copy-start.2
  103.0 10.2 %copy-start.3 = (bf16[16,16,16,128]{3,2,1,0:T(8,128)(2,1)S(1)}, bf16[16,16,16,128]{3,2,1,0:T(8,128)(2,1)}, u32[]{:S(2)}) copy-start(bf16[16,16,16,128]{3,2,1,0:T(8,128)(2,1)} %copy-done.2) | copy-start | bytes 3145732
  103.0 32.7 %all-to-all-start.2 = ((f32[32,64,128]{2,1,0:T(8,128)}), f32[32,64,128]{2,1,0:T(8,128)S(1)}, u32[]{:S(2)}, u32[]{:S(2)}) async-start(f32[32,64,128]{2,1,0:T(8,128)} %bitcast.34), calls=%async_computation.2 | async-start | bytes 2097152 | tf_op jit(solution)/shard_map/all_to_all | solution.py:242
  110.5 25.7 %collective-permute-start.13 = (bf16[16,16,16,128]{3,2,1,0:T(8,128)(2,1)}, bf16[16,16,16,128]{3,2,1,0:T(8,128)(2,1)S(1)}, u32[]{:S(2)}, u32[]{:S(2)}) collective-permute-start(bf16[16,16,16,128]{3,2,1,0:T(8,128)(2,1)} %collective-permute-done.8.b_ref.refs_4_.refs_3_), channel_id=1, source_target_pairs={{0,7},{1,0},{2,1},{3,2},{4,3},{5,4},{6,5},{7,6},{8,15},{9,8},{10,9... | collective-permute-start | bytes 3145736 | tf_op jit(solution)/shard_map/ppermute | solution.py:218
  113.2 26.2 %collective-permute-start.14 = (bf16[16,16,16,128]{3,2,1,0:T(8,128)(2,1)S(1)}, bf16[16,16,16,128]{3,2,1,0:T(8,128)(2,1)}, u32[]{:S(2)}, u32[]{:S(2)}) collective-permute-start(bf16[16,16,16,128]{3,2,1,0:T(8,128)(2,1)S(1)} %copy-done.3), channel_id=1, source_target_pairs={{0,1},{1,2},{2,3},{3,4},{4,5},{5,6},{6,7},{7,0},{8,9},{9,10},{10,1... | collective-permute-start | bytes 3145736 | tf_op jit(solution)/shard_map/ppermute | solution.py:218
  136.3 3.2 %copy-start.5 = (bf16[16,16,16,128]{3,2,1,0:T(8,128)(2,1)}, bf16[16,16,16,128]{3,2,1,0:T(8,128)(2,1)S(1)}, u32[]{:S(2)}) copy-start(bf16[16,16,16,128]{3,2,1,0:T(8,128)(2,1)S(1)} %collective-permute-done.13.refs_3_) | copy-start | bytes 3145732
  147.4 15.4 %all-to-all-start.3 = ((bf16[32,64,128]{2,1,0:T(8,128)(2,1)}), bf16[32,64,128]{2,1,0:T(8,128)(2,1)S(1)}, u32[]{:S(2)}, u32[]{:S(2)}) async-start(bf16[32,64,128]{2,1,0:T(8,128)(2,1)} %bitcast.35), calls=%async_computation.3 | async-start | bytes 1048576 | tf_op jit(solution)/shard_map/all_to_all | solution.py:242
  154.8 13.0 %collective-permute-start.15 = (f32[64,128]{1,0:T(8,128)S(1)}, f32[64,128]{1,0:T(8,128)S(1)}, u32[]{:S(2)}, u32[]{:S(2)}) collective-permute-start(f32[64,128]{1,0:T(8,128)S(1)} %broadcast_multiply_fusion.1), channel_id=1, source_target_pairs={{0,0},{1,33},{2,66},{3,99},{4,132},{5,165},{6,198},{7,231},{16,8},... | collective-permute-start | bytes 98312 | tf_op jit(solution)/shard_map/ppermute | solution.py:218
  162.9 10.3 %collective-permute-start.16 = (f32[64,128]{1,0:T(8,128)S(1)}, f32[64,128]{1,0:T(8,128)S(1)}, u32[]{:S(2)}, u32[]{:S(2)}) collective-permute-start(f32[64,128]{1,0:T(8,128)S(1)} %broadcast_multiply_fusion), channel_id=1, source_target_pairs={{0,38},{1,71},{2,96},{3,129},{4,162},{5,195},{6,228},{7,5},{16,46}... | collective-permute-start | bytes 98312 | tf_op jit(solution)/shard_map/ppermute | solution.py:218
  165.8 7.4 %collective-permute-start.17 = (f32[64,128]{1,0:T(8,128)S(1)}, f32[64,128]{1,0:T(8,128)S(1)}, u32[]{:S(2)}, u32[]{:S(2)}) collective-permute-start(f32[64,128]{1,0:T(8,128)S(1)} %broadcast_multiply_fusion.1), channel_id=1, source_target_pairs={{8,0},{9,33},{10,66},{11,99},{12,132},{13,165},{14,198},{15,231},{... | collective-permute-start | bytes 98312 | tf_op jit(solution)/shard_map/ppermute | solution.py:218
  166.5 12.2 %collective-permute-start.18 = (f32[64,128]{1,0:T(8,128)S(1)}, f32[64,128]{1,0:T(8,128)S(1)}, u32[]{:S(2)}, u32[]{:S(2)}) collective-permute-start(f32[64,128]{1,0:T(8,128)S(1)} %broadcast_multiply_fusion), channel_id=1, source_target_pairs={{8,226},{9,3},{10,36},{11,69},{12,102},{13,135},{14,160},{15,193},... | collective-permute-start | bytes 98312 | tf_op jit(solution)/shard_map/ppermute | solution.py:218

commit v3 on v2

--- a/solution.py
+++ b/solution.py
@@ -5,8 +5,16 @@
 from jax.experimental.pallas import tpu as pltpu
 from jax.sharding import Mesh, PartitionSpec as P
 
-EARLY = ((0, 0, 0), (0, 1, 0), (0, 0, 1), (0, 1, 1), (0, 0, -1), (0, 1, -1), (-1, 1, 1), (1, 0, -1))
-LATE = ((-2, 0, 1), (2, 1, -1), (0, 0, 2), (-1, 1, 2), (-2, 0, 2), (0, 1, -2), (1, 0, -2), (2, 1, -2))
+TILES = (
+    ((0, 0), (0, 0)),
+    ((0, 1), (0, 1)),
+    ((0, -1), (0, -1)),
+    ((0, 2), (-1, 1)),
+    ((1, -1), (0, -2)),
+    ((-2, 1), (-1, 2)),
+    ((1, -2), (2, -1)),
+    ((-2, 2), (2, -2)),
+)
 B = 64
 TERMS = 8
 VMEM_LIMIT = 60 * 2**20
@@ -67,7 +75,7 @@
         choose_kernel,
         in_specs=[SMEM, SMEM, pl.BlockSpec(memory_space=pltpu.VMEM)],
         out_shape=jax.ShapeDtypeStruct((64, B, 2 * B), BF16),
-        cost_estimate=pl.CostEstimate(flops=2**21, bytes_accessed=3 * 2**19, transcendentals=0),
+        cost_estimate=pl.CostEstimate(flops=120 * 256**3, bytes_accessed=3 * 2**19, transcendentals=0),
     )(occ_list, virt_list, held)
 
 
@@ -109,7 +117,7 @@
             jax.ShapeDtypeStruct((16, TERMS, 16, 256), BF16),
             jax.ShapeDtypeStruct((256, TERMS * 256), BF16),
         ],
-        cost_estimate=pl.CostEstimate(flops=2**28, bytes_accessed=3 * 2**20, transcendentals=0),
+        cost_estimate=pl.CostEstimate(flops=200 * 256**3, bytes_accessed=3 * 2**20, transcendentals=0),
     )(term_count, blocks)
 
 
@@ -148,13 +156,17 @@
         out_shape=jax.ShapeDtypeStruct((256, 4096), BF16),
         scratch_shapes=[pltpu.VMEM((16, TERMS, 16, 16, 256), BF16)],
         compiler_params=pltpu.CompilerParams(vmem_limit_bytes=VMEM_LIMIT),
-        cost_estimate=pl.CostEstimate(flops=2 * 256 * 256**3, bytes_accessed=6 * 2**20, transcendentals=0),
+        cost_estimate=pl.CostEstimate(flops=512 * 256**3, bytes_accessed=6 * 2**20, transcendentals=0),
     )(first, second, w1, w2)
 
 
-def tiles(images, columns, jobs, kind, base=None, given=()):
+def tiles(images, columns, jobs, base=None, given=()):
     count, width = len(images), len(columns)
     rows_of = [len(parts) * 128 for _, parts in jobs]
+
+    def at(place, side):
+        tile, half = place
+        return tile // 2, slice(2 * side, 2 * side + 2), tile % 2, slice(half * B, (half + 1) * B)
 
     def kernel(*refs):
         image_refs, column_refs = refs[:count], refs[count:count + width]
@@ -167,14 +179,7 @@
             part = jnp.dot(
                 jnp.concatenate(rows, axis=0), jnp.concatenate(block, axis=1), preferred_element_type=F32
             )
-
-            @pl.when(step == 0)
-            def _():
-                sum_ref[...] = part
-
-            @pl.when(step > 0)
-            def _():
-                sum_ref[...] += part
+            sum_ref[...] = jnp.where(step == 0, 0.0, sum_ref[...]) + part
 
         @pl.when(step == 3)
         def _():
@@ -182,12 +187,11 @@
                 for r, (_, _, place) in enumerate(parts):
                     for n, (_, side) in enumerate(held):
                         tile = sum_ref[r * 128:(r + 1) * 128, n * 128:(n + 1) * 128].T
-                        o_ref[place // 2, 2 * side:2 * side + 2, place % 2] = tile.astype(kind).reshape(2, B, 128)
+                        o_ref[at(place, side)] = tile.astype(BF16).reshape(2, B, 128)
             for place, side in given:
-                at = (place // 2, slice(2 * side, 2 * side + 2), place % 2)
-                o_ref[at] = refs[count + width][at]
-
-    whole = pl.BlockSpec((4, 4, 2, B, 128), lambda i: (0, 0, 0, 0, 0))
+                o_ref[at(place, side)] = refs[count + width][at(place, side)]
+
+    whole = pl.BlockSpec((4, 4, 2, 2 * B, 128), lambda i: (0, 0, 0, 0, 0))
     flops = sum(2 * 4096 * r * 128 * len(held) for r, (held, _) in zip(rows_of, jobs))
     return pl.pallas_call(
         kernel,
@@ -196,11 +200,11 @@
         + [pl.BlockSpec((4, 16, 16, 128), lambda i: (i, 0, 0, 0))] * width
         + ([] if base is None else [whole]),
         out_specs=whole,
-        out_shape=jax.ShapeDtypeStruct((4, 4, 2, B, 128), kind),
+        out_shape=jax.ShapeDtypeStruct((4, 4, 2, 2 * B, 128), BF16),
         scratch_shapes=[pltpu.VMEM((r, 128 * len(held)), F32) for r, (held, _) in zip(rows_of, jobs)],
         compiler_params=pltpu.CompilerParams(vmem_limit_bytes=VMEM_LIMIT),
         cost_estimate=pl.CostEstimate(
-            flops=flops, bytes_accessed=(2 * count + width + 1) * 2**20, transcendentals=0
+            flops=flops, bytes_accessed=(2 * count + width + 2) * 2**20, transcendentals=0
         ),
     )(*images, *columns, *([] if base is None else [base]))
 
@@ -230,34 +234,25 @@
     return lax.all_to_all(jnp.broadcast_to(block[None], (count,) + block.shape), axis, 0, 0)
 
 
-def along_z(block):
-    z = lax.axis_index("z")
-    found = [block]
-    for n in range(1, 8):
-        found.append(moved(block, lambda y, x, c, z: (y, x, c, (z - n) % 8)))
-    return jnp.roll(jnp.stack(found), z, axis=0)
-
-
 def add_up(pieces):
-    arrived = lax.all_to_all(pieces.reshape(32, B, 128), ORB, 0, 0)
-    return arrived.astype(F32).sum(0) * (0.25 / B)
-
-
-def placed(total, group):
-    def target(y, x, c, z):
-        row, _, col = group[y * 2 + c]
-        orb = ((z + col) % 8) * 4 + x
-        return orb // 8, orb // 2 % 4, orb % 2, (z + row) % 8
-
-    halves = [[p for p in PLACES if group[p[0] * 2 + p[2]][1] == half] for half in range(2)]
-    return [moved(total, target, places) for places in halves]
+    arrived = lax.all_to_all(pieces.reshape(32, 2 * B, 128), ORB, 0, 0)
+    total = arrived.astype(F32).sum(0) * (0.25 / B)
+
+    def send(half):
+        def target(y, x, c, z):
+            row, col = TILES[y * 2 + c][half]
+            orb = ((z + col) % 8) * 4 + x
+            return orb // 8, orb // 2 % 4, orb % 2, (z + row) % 8
+
+        return moved(total[half * B:(half + 1) * B], target)
+
+    return jnp.concatenate([send(0), send(1)], axis=1).T
 
 
 def body(three_centre, occ_blocks, virt_blocks, occ_list, virt_list, term_count):
     both = jnp.concatenate([occ_blocks[0], virt_blocks[0]], axis=1)
     own = order_rows(three_centre[0])
-    column = along_z(both)
-    own, column = lax.optimization_barrier((own, column))
+    column = spread(both, "z", 8)
     below_first, above_first = up(own[0]), down(own[1])
     below_last, above_last = up(own[1]), down(own[0])
     far_below_first, far_above_first = up(below_first), down(above_first)
@@ -271,46 +266,46 @@
     image, below_last, above_last = lax.optimization_barrier((image, below_last, above_last))
     far_below_last, far_above_last = up(below_last), down(above_last)
     near = image_rows(below_last, above_last, w1, w2)
-    early = tiles(
+    above, below = [(2, 0), (3, 1)], [(4, 0), (5, 1)]
+    columns = [own[0], own[1], above_last, above_first, below_first, below_last]
+    sums = tiles(
         [image, near],
-        [own[0], own[1], above_last, above_first, below_first, below_last],
+        columns,
         [
-            ([(0, 0), (1, 1)], [(0, 0, 0), (0, 1, 1)]),
-            ([(2, 0), (3, 1)], [(0, 0, 2), (0, 1, 3), (1, 0, 6)]),
-            ([(4, 0), (5, 1)], [(0, 0, 4), (0, 1, 5), (1, 1, 7)]),
+            ([(0, 0), (1, 1)], [(0, 0, (0, 0)), (0, 1, (0, 1))]),
+            (above, [(0, 0, (1, 0)), (0, 1, (1, 1)), (1, 0, (3, 1))]),
+            (below, [(0, 0, (2, 0)), (0, 1, (2, 1)), (1, 1, (4, 0))]),
         ],
-        F32,
     )
-    early, far_below_first, far_above_first = lax.optimization_barrier((early, far_below_first, far_above_first))
-    early = add_up(early)
+    early = [(0, 0), (0, 1), (1, 0), (1, 1), (3, 1), (2, 0), (2, 1), (4, 0)]
+    given = [(place, side) for place in early for side in range(2)]
+    sums, far_below_first, far_above_first = lax.optimization_barrier((sums, far_below_first, far_above_first))
     far = image_rows(far_below_first, far_above_first, w1, w2)
-    late_above = [(0, 0, 2), (1, 0, 3), (2, 0, 4)]
-    late_below = [(0, 1, 5), (1, 1, 6), (2, 1, 7)]
-    late = tiles(
+    far_above = [(0, 0, (3, 0)), (1, 0, (5, 1)), (2, 0, (7, 0))]
+    far_below = [(0, 1, (4, 1)), (1, 1, (6, 0)), (2, 1, (7, 1))]
+    sums = tiles(
         [image, near, far],
-        [above_last, above_first, below_first, below_last, far_above_first, far_below_first],
+        columns[2:] + [far_above_first, far_below_first],
         [
-            ([(0, 0), (1, 1)], [(2, 0, 0)]),
-            ([(2, 0), (3, 1)], [(2, 1, 1)]),
-            ([(4, 1)], late_above),
-            ([(5, 0)], late_below),
+            ([(0, 0), (1, 1)], [(2, 0, (5, 0))]),
+            ([(2, 0), (3, 1)], [(2, 1, (6, 1))]),
+            ([(4, 1)], far_above),
+            ([(5, 0)], far_below),
         ],
-        BF16,
+        sums,
+        given,
     )
-    late, early, far_above_last, far_below_last = lax.optimization_barrier(
-        (late, early, far_above_last, far_below_last)
-    )
-    early = placed(early, EARLY)
-    late = tiles(
+    given = given + [((5, 0), 0), ((5, 0), 1), ((6, 1), 0), ((6, 1), 1)]
+    given = given + [(place, 1) for _, _, place in far_above] + [(place, 0) for _, _, place in far_below]
+    sums, far_above_last, far_below_last = lax.optimization_barrier((sums, far_above_last, far_below_last))
+    sums = tiles(
         [image, near, far],
         [far_above_last, far_below_last],
-        [([(0, 0)], late_above), ([(1, 1)], late_below)],
-        BF16,
-        late,
-        [(0, 0), (0, 1), (1, 0), (1, 1), (2, 1), (3, 1), (4, 1), (5, 0), (6, 0), (7, 0)],
+        [([(0, 0)], far_above), ([(1, 1)], far_below)],
+        sums,
+        given,
     )
-    late = placed(add_up(late), LATE)
-    return jnp.concatenate([e + l for e, l in zip(early, late)], axis=1).T
+    return add_up(sums)
 
 
 def solution(mesh):

time: 183 us -> 165 us (0.902); the launches traced: 179 us -> 164 us
  blocking collectives: 0 us -> 38 us
  starting transfers between devices: 62.8 us -> 27.5 us
  waiting for transfers between devices: 35.8 us -> 25.3 us
  Pallas kernels: 75.1 us -> 70 us
  local copies, waits for them, and re-layouts: 3.93 us -> 1.78 us
    all_to_all x0 -> x2, blocking collectives: none -> 38 us  [the longest x1 20.6 us: add_up(): arrived = lax.all_to_all(pieces.reshape(32, 2 * B, 128), ORB, 0, 0)]
    ppermute x19 -> x10, starting transfers between devices: 38.3 us -> 17.9 us  [moved(): lax.ppermute(value, ALL, [(number(*p), number(*target(*p))) for p in plac...]
    all_to_all x2 -> x0, starting transfers between devices: 14.9 us -> none  [add_up(): arrived = lax.all_to_all(pieces.reshape(32, B, 128), ORB, 0, 0)]
    pallas_call x3, Pallas kernels: 26.9 us -> 21.9 us  [tiles(): pl.pallas_call(kernel, grid=(4,), in_specs=[pl.BlockSpec((256, 1024), lam...]
    ppermute x19 -> x10, waiting for transfers between devices: 29.6 us -> 25.3 us  [moved(): lax.ppermute(value, ALL, [(number(*p), number(*target(*p))) for p in plac...]
    all_to_all x2 -> x0, waiting for transfers between devices: 4.28 us -> none  [add_up(): arrived = lax.all_to_all(pieces.reshape(32, B, 128), ORB, 0, 0)]
    unnamed x26 -> x8, local copies, waits for them, and re-layouts: 2.97 us -> 0.83 us
    all_to_all x1, waiting for transfers between devices: 1.88 us -> 0.01 us  [spread(): lax.all_to_all(jnp.broadcast_to(block[None], (count,) + block.shape), axi...]
  transfers between devices with their start and end apart: 23 -> 12, of which waited for: 10 -> 5; matrix products, arithmetic and copies ran while one was open for 0% -> 0% of each run, Pallas kernels for 37% -> 39%
where the time goes in v3:
time: 165 us; the launch traced here: 164 us
  Pallas kernels  70 us (42%)
  blocking collectives  38 us (23%)
  starting transfers between devices  27.5 us (17%)
  waiting for transfers between devices  25.3 us (15%)
  local copies, waits for them, and re-layouts  1.78 us (1%)
    pallas_call x3, Pallas kernels, image_rows(): pl.pallas_call(image_kernel, grid=(4,), in_specs=[spec, spec, pl.BlockSpe...  37.9 us
    ppermute x10, waiting for transfers between devices, moved(): lax.ppermute(value, ALL, [(number(*p), number(*target(*p))) for p in plac...  25.3 us
    pallas_call x3, Pallas kernels, tiles(): pl.pallas_call(kernel, grid=(4,), in_specs=[pl.BlockSpec((256, 1024), lam...  21.9 us
    all_to_all x1, blocking collectives, add_up(): arrived = lax.all_to_all(pieces.reshape(32, 2 * B, 128), ORB, 0, 0)  20.6 us
    ppermute x10, starting transfers between devices, moved(): lax.ppermute(value, ALL, [(number(*p), number(*target(*p))) for p in plac...  17.9 us
    all_to_all x1, blocking collectives, spread(): lax.all_to_all(jnp.broadcast_to(block[None], (count,) + block.shape), axi...  17.4 us
    all_to_all x1, starting transfers between devices, body(): arrived = lax.all_to_all(chosen.reshape(8, 8, B, 2 * B), ('x', 'c'), 0, 0)  4.8 us
    all_to_all x1, starting transfers between devices, spread(): lax.all_to_all(jnp.broadcast_to(block[None], (count,) + block.shape), axi...  4.8 us
  transfers between devices with their start and end apart: 12, of which 5 were waited for; matrix products, arithmetic and copies ran while one was open for 0% of the time, Pallas kernels for 39%

profile of v3, /device:TPU:20, one launch (start us, length us, event | category | flops | bytes accessed | tf_op | source)
XLA Modules:
  0.0 164.3 jit_solution(3152953650872723704)
XLA Ops:
  0.0 0.8 pad_maximum_fusion
  0.8 17.4 %all_to_all.20 = bf16[8,64,128]{2,1,0:T(8,128)(2,1)S(1)} all-to-all(bf16[8,64,128]{2,1,0:T(8,128)(2,1)S(1)} %broadcast_in_dim.4), channel_id=1, replica_groups=mesh['y'=4,'x'=4,'c'=2,'z'=8] {'z'}, dimensions={0} | all-to-all | bytes 262144 | tf_op jit(solution)/shard_map/all_to_all | solution.py:234
  18.2 0.9 broadcast_in_dim.5
  19.1 4.8 %all-to-all-start.1 = ((bf16[4,8,64,128]{3,2,1,0:T(8,128)(2,1)}), bf16[4,8,64,128]{3,2,1,0:T(8,128)(2,1)S(1)}, u32[]{:S(2)}, u32[]{:S(2)}) async-start(bf16[4,8,64,128]{3,2,1,0:T(8,128)(2,1)} %broadcast_in_dim.5), calls=%async_computation.1 | async-start | bytes 1048576 | tf_op jit(solution)/shard_map/all_to_all | solution.py:234
  23.9 3.3 %shard_map.64 = (bf16[16,16,16,128]{3,2,1,0:T(8,128)(2,1)}, bf16[16,16,16,128]{3,2,1,0:T(8,128)(2,1)}) custom-call(bf16[256,4096]{1,0:T(8,128)(2,1)} %bitcast.9), custom_call_target="tpu_custom_call" | custom-call | flops 536870912 | bytes 4194304 | tf_op jit(solution)/shard_map/pallas_call | solution.py:43
  27.2 2.0 %collective-permute-start.3 = (bf16[16,16,16,128]{3,2,1,0:T(8,128)(2,1)}, bf16[16,16,16,128]{3,2,1,0:T(8,128)(2,1)S(1)}, u32[]{:S(2)}, u32[]{:S(2)}) collective-permute-start(bf16[16,16,16,128]{3,2,1,0:T(8,128)(2,1)} %get-tuple-element.18.a_ref.refs_2_), channel_id=1, source_target_pairs={{0,1},{1,2},{2,3},{3,4},{4,5},{5,6},{6,7},{7,0},{8,9},{9,10},{10,1... | collective-permute-start | bytes 3145736 | tf_op jit(solution)/shard_map/ppermute | solution.py:222
  29.2 0.8 copy-done.3
  30.0 2.6 %shard_map.65 = bf16[64,64,128]{2,1,0:T(8,128)(2,1)} custom-call(s32[256]{0:T(256)} %occ_list.1, s32[256]{0:T(256)} %virt_list.1, bf16[32,64,128]{2,1,0:T(8,128)(2,1)} %bitcast.11), custom_call_target="tpu_custom_call" | custom-call | flops 2013265920 | bytes 1572864 | tf_op jit(solution)/shard_map/pallas_call | solution.py:74
  32.6 4.8 %all-to-all-start.2 = ((bf16[8,8,64,128]{3,2,1,0:T(8,128)(2,1)}), bf16[8,8,64,128]{3,2,1,0:T(8,128)(2,1)}, u32[]{:S(2)}, u32[]{:S(2)}) async-start(bf16[8,8,64,128]{3,2,1,0:T(8,128)(2,1)} %bitcast.10), calls=%async_computation.2 | async-start | bytes 2097152 | tf_op jit(solution)/shard_map/all_to_all | solution.py:262
  37.4 0.4 collective-permute-start
  37.8 2.9 %collective-permute-start.1 = (bf16[16,16,16,128]{3,2,1,0:T(8,128)(2,1)}, bf16[16,16,16,128]{3,2,1,0:T(8,128)(2,1)}, u32[]{:S(2)}, u32[]{:S(2)}) collective-permute-start(bf16[16,16,16,128]{3,2,1,0:T(8,128)(2,1)} %get-tuple-element.18.a_ref.refs_2_), channel_id=1, source_target_pairs={{0,7},{1,0},{2,1},{3,2},{4,3},{5,4},{6,5},{7,6},{8,15},{9,8},{10,9... | collective-permute-start | bytes 3145736 | tf_op jit(solution)/shard_map/ppermute | solution.py:222
  40.7 14.0 %collective-permute-done.3.refs_6_.refs_5_ = bf16[16,16,16,128]{3,2,1,0:T(8,128)(2,1)S(1)} collective-permute-done((bf16[16,16,16,128]{3,2,1,0:T(8,128)(2,1)}, bf16[16,16,16,128]{3,2,1,0:T(8,128)(2,1)S(1)}, u32[]{:S(2)}, u32[]{:S(2)}) %collective-permute-start.3) | collective-permute-done | bytes 1048608 | tf_op jit(solution)/shard_map/ppermute | solution.py:222
  54.7 0.8 collective-permute-start.4
  55.5 2.4 %collective-permute-start.5 = (bf16[16,16,16,128]{3,2,1,0:T(8,128)(2,1)S(1)}, bf16[16,16,16,128]{3,2,1,0:T(8,128)(2,1)}, u32[]{:S(2)}, u32[]{:S(2)}) collective-permute-start(bf16[16,16,16,128]{3,2,1,0:T(8,128)(2,1)S(1)} %collective-permute-done.2.refs_5_.refs_4_), channel_id=1, source_target_pairs={{0,7},{1,0},{2,1},{3,2},{4,3},{5,4},{6,5},{7,6},{8,15},{9,8},{10,9... | collective-permute-start | bytes 3145736 | tf_op jit(solution)/shard_map/ppermute | solution.py:222
  58.0 4.4 %shard_map.66 = (bf16[16,8,16,256]{3,2,1,0:T(8,128)(2,1)}, bf16[256,2048]{1,0:T(8,128)(2,1)}) custom-call(s32[32]{0:T(128)} %count_ref.1, bf16[8,8,64,128]{3,2,1,0:T(8,128)(2,1)} %all-to-all-done.2.b_ref), custom_call_target="tpu_custom_call" | custom-call | flops 3355443200 | bytes 3145728 | tf_op jit(solution)/shard_map/pallas_call | solution.py:113
  62.3 12.6 %shard_map.67.refs_0_ = bf16[256,4096]{1,0:T(8,128)(2,1)} custom-call(bf16[16,16,16,128]{3,2,1,0:T(8,128)(2,1)} %get-tuple-element.18.a_ref.refs_2_, bf16[16,16,16,128]{3,2,1,0:T(8,128)(2,1)} %get-tuple-element.19.b_ref.refs_3_, bf16[16,8,16,256]{3,2,1,0:T(8,128)(2,1)} %get-tuple-element.20.w1_ref, bf16[256,2048]{1,0:T(8,128)(2,1)} %get-tuple-element.21.w2_ref), custom_call_target="tpu_custom_call" | custom-call | flops 8589934592 | bytes 6291456 | tf_op jit(solution)/shard_map/pallas_call | solution.py:146
  74.9 2.2 %collective-permute-done.a_ref.refs_7_.refs_6_ = bf16[16,16,16,128]{3,2,1,0:T(8,128)(2,1)S(1)} collective-permute-done((bf16[16,16,16,128]{3,2,1,0:T(8,128)(2,1)}, bf16[16,16,16,128]{3,2,1,0:T(8,128)(2,1)S(1)}, u32[]{:S(2)}, u32[]{:S(2)}) %collective-permute-start) | collective-permute-done | bytes 1048608 | tf_op jit(solution)/shard_map/ppermute | solution.py:222
  77.2 0.1 collective-permute-start.6
  77.3 1.9 %collective-permute-start.7 = (bf16[16,16,16,128]{3,2,1,0:T(8,128)(2,1)S(1)}, bf16[16,16,16,128]{3,2,1,0:T(8,128)(2,1)}, u32[]{:S(2)}, u32[]{:S(2)}) collective-permute-start(bf16[16,16,16,128]{3,2,1,0:T(8,128)(2,1)S(1)} %collective-permute-done.a_ref.refs_7_.refs_6_), channel_id=1, source_target_pairs={{0,1},{1,2},{2,3},{3,4},{4,5},{5,6},{6,7},{7,0},{8,9},{9,10},{10,1... | collective-permute-start | bytes 3145736 | tf_op jit(solution)/shard_map/ppermute | solution.py:222
  79.2 12.6 %shard_map.68.refs_1_ = bf16[256,4096]{1,0:T(8,128)(2,1)} custom-call(bf16[16,16,16,128]{3,2,1,0:T(8,128)(2,1)} %copy-done.2, bf16[16,16,16,128]{3,2,1,0:T(8,128)(2,1)} %collective-permute-done.1.b_ref.refs_4_.refs_3_, bf16[16,8,16,256]{3,2,1,0:T(8,128)(2,1)} %get-tuple-element.20.w1_ref, bf16[256,2048]{1,0:T(8,128)(2,1)} %get-tuple-element.21.w2_ref), custom_call_target="tpu_custom_call" | custom-call | flops 8589934592 | bytes 6291456 | tf_op jit(solution)/shard_map/pallas_call | solution.py:146
  91.8 7.0 %shard_map.69.refs_9_ = bf16[4,4,2,128,128]{4,3,2,1,0:T(8,128)(2,1)} custom-call(bf16[256,4096]{1,0:T(8,128)(2,1)} %shard_map.67.refs_0_, bf16[256,4096]{1,0:T(8,128)(2,1)} %shard_map.68.refs_1_, bf16[16,16,16,128]{3,2,1,0:T(8,128)(2,1)} %get-tuple-element.18.a_ref.refs_2_, bf16[16,16,16,128]{3,2,1,0:T(8,128)(2,1)} %get-tuple-element.19.b_ref.refs_3_, ...), custom_call_target="tpu_custom_call" | custom-call | flops 2147483648 | bytes 12582912 | tf_op jit(solution)/shard_map/pallas_call | solution.py:196
  98.8 1.0 collective-permute-done.4.a_ref.refs_8_
  99.8 12.7 %shard_map.70.refs_2_ = bf16[256,4096]{1,0:T(8,128)(2,1)} custom-call(bf16[16,16,16,128]{3,2,1,0:T(8,128)(2,1)} %collective-permute-done.4.a_ref.refs_8_, bf16[16,16,16,128]{3,2,1,0:T(8,128)(2,1)} %collective-permute-done.5.b_ref.refs_7_, bf16[16,8,16,256]{3,2,1,0:T(8,128)(2,1)} %get-tuple-element.20.w1_ref, bf16[256,2048]{1,0:T(8,128)(2,1)} %get-tuple-element.21.w2_ref), custom_call_target="tpu_custom_call" | custom-call | flops 8589934592 | bytes 6291456 | tf_op jit(solution)/shard_map/pallas_call | solution.py:146
  112.4 8.2 %shard_map.71.refs_5_ = bf16[4,4,2,128,128]{4,3,2,1,0:T(8,128)(2,1)} custom-call(bf16[256,4096]{1,0:T(8,128)(2,1)} %shard_map.67.refs_0_, bf16[256,4096]{1,0:T(8,128)(2,1)} %shard_map.68.refs_1_, bf16[256,4096]{1,0:T(8,128)(2,1)} %shard_map.70.refs_2_, bf16[16,16,16,128]{3,2,1,0:T(8,128)(2,1)} %collective-permute-done.1.b_ref.refs_4_.refs_3_, ...), custom_call_target="tpu_custom_call" | custom-call | flops 1342177280 | bytes 14680064 | tf_op jit(solution)/shard_map/pallas_call | solution.py:196
  120.6 6.8 %shard_map.72 = bf16[4,4,2,128,128]{4,3,2,1,0:T(8,128)(2,1)} custom-call(bf16[256,4096]{1,0:T(8,128)(2,1)} %shard_map.67.refs_0_, bf16[256,4096]{1,0:T(8,128)(2,1)} %shard_map.68.refs_1_, bf16[256,4096]{1,0:T(8,128)(2,1)} %shard_map.70.refs_2_, bf16[16,16,16,128]{3,2,1,0:T(8,128)(2,1)} %collective-permute-done.6.refs_3_, ...), custom_call_target="tpu_custom_call" | custom-call | flops 805306368 | bytes 10485760 | tf_op jit(solution)/shard_map/pallas_call | solution.py:196
  127.4 20.6 %all_to_all.21 = bf16[32,128,128]{2,1,0:T(8,128)(2,1)S(1)} all-to-all(bf16[32,128,128]{2,1,0:T(8,128)(2,1)} %bitcast.8), channel_id=1, replica_groups=mesh['y'=4,'x'=4,'c'=2,'z'=8] {'y','x','c'}, dimensions={0} | all-to-all | bytes 2097152 | tf_op jit(solution)/shard_map/all_to_all | solution.py:238
  148.0 0.2 convert_reduce_fusion
  148.2 4.1 %collective-permute-start.8 = (f32[64,128]{1,0:T(8,128)S(1)}, f32[64,128]{1,0:T(8,128)S(1)}, u32[]{:S(2)}, u32[]{:S(2)}) collective-permute-start(f32[64,128]{1,0:T(8,128)S(1)} %get-tuple-element.31), channel_id=1, source_target_pairs={{0,0},{1,33},{2,66},{3,99},{4,132},{5,165},{6,198},{7,231},{8,32},... | collective-permute-start | bytes 98312 | tf_op jit(solution)/shard_map/ppermute | solution.py:222
  152.3 3.3 %collective-permute-start.9 = (f32[64,128]{1,0:T(8,128)S(1)}, f32[64,128]{1,0:T(8,128)S(1)}, u32[]{:S(2)}, u32[]{:S(2)}) collective-permute-start(f32[64,128]{1,0:T(8,128)S(1)} %get-tuple-element.32), channel_id=1, source_target_pairs={{0,0},{1,33},{2,66},{3,99},{4,132},{5,165},{6,198},{7,231},{8,32},... | collective-permute-start | bytes 98312 | tf_op jit(solution)/shard_map/ppermute | solution.py:222
  155.6 2.9 %collective-permute-done.8 = f32[64,128]{1,0:T(8,128)S(1)} collective-permute-done((f32[64,128]{1,0:T(8,128)S(1)}, f32[64,128]{1,0:T(8,128)S(1)}, u32[]{:S(2)}, u32[]{:S(2)}) %collective-permute-start.8) | collective-permute-done | bytes 32800 | tf_op jit(solution)/shard_map/ppermute | solution.py:222
  158.5 5.2 %collective-permute-done.9 = f32[64,128]{1,0:T(8,128)S(1)} collective-permute-done((f32[64,128]{1,0:T(8,128)S(1)}, f32[64,128]{1,0:T(8,128)S(1)}, u32[]{:S(2)}, u32[]{:S(2)}) %collective-permute-start.9) | collective-permute-done | bytes 32800 | tf_op jit(solution)/shard_map/ppermute | solution.py:222
  163.7 0.6 maximum_bitcast_fusion
  (18 shorter events, 0.1 us)
Async XLA Ops:
  19.1 10.1 %all-to-all-start.1 = ((bf16[4,8,64,128]{3,2,1,0:T(8,128)(2,1)}), bf16[4,8,64,128]{3,2,1,0:T(8,128)(2,1)S(1)}, u32[]{:S(2)}, u32[]{:S(2)}) async-start(bf16[4,8,64,128]{3,2,1,0:T(8,128)(2,1)} %broadcast_in_dim.5), calls=%async_computation.1 | async-start | bytes 1048576 | tf_op jit(solution)/shard_map/all_to_all | solution.py:234
  27.2 28.3 %collective-permute-start.2 = (bf16[16,16,16,128]{3,2,1,0:T(8,128)(2,1)}, bf16[16,16,16,128]{3,2,1,0:T(8,128)(2,1)S(1)}, u32[]{:S(2)}, u32[]{:S(2)}) collective-permute-start(bf16[16,16,16,128]{3,2,1,0:T(8,128)(2,1)} %get-tuple-element.19.b_ref.refs_3_), channel_id=1, source_target_pairs={{0,7},{1,0},{2,1},{3,2},{4,3},{5,4},{6,5},{7,6},{8,15},{9,8},{10,9... | collective-permute-start | bytes 3145736 | tf_op jit(solution)/shard_map/ppermute | solution.py:222
  27.2 27.5 %collective-permute-start.3 = (bf16[16,16,16,128]{3,2,1,0:T(8,128)(2,1)}, bf16[16,16,16,128]{3,2,1,0:T(8,128)(2,1)S(1)}, u32[]{:S(2)}, u32[]{:S(2)}) collective-permute-start(bf16[16,16,16,128]{3,2,1,0:T(8,128)(2,1)} %get-tuple-element.18.a_ref.refs_2_), channel_id=1, source_target_pairs={{0,1},{1,2},{2,3},{3,4},{4,5},{5,6},{6,7},{7,0},{8,9},{9,10},{10,1... | collective-permute-start | bytes 3145736 | tf_op jit(solution)/shard_map/ppermute | solution.py:222
  29.2 0.8 copy-start.3
  32.6 25.3 %all-to-all-start.2 = ((bf16[8,8,64,128]{3,2,1,0:T(8,128)(2,1)}), bf16[8,8,64,128]{3,2,1,0:T(8,128)(2,1)}, u32[]{:S(2)}, u32[]{:S(2)}) async-start(bf16[8,8,64,128]{3,2,1,0:T(8,128)(2,1)} %bitcast.10), calls=%async_computation.2 | async-start | bytes 2097152 | tf_op jit(solution)/shard_map/all_to_all | solution.py:262
  37.4 39.7 %collective-permute-start = (bf16[16,16,16,128]{3,2,1,0:T(8,128)(2,1)}, bf16[16,16,16,128]{3,2,1,0:T(8,128)(2,1)S(1)}, u32[]{:S(2)}, u32[]{:S(2)}) collective-permute-start(bf16[16,16,16,128]{3,2,1,0:T(8,128)(2,1)} %get-tuple-element.19.b_ref.refs_3_), channel_id=1, source_target_pairs={{0,1},{1,2},{2,3},{3,4},{4,5},{5,6},{6,7},{7,0},{8,9},{9,10},{10,1... | collective-permute-start | bytes 3145736 | tf_op jit(solution)/shard_map/ppermute | solution.py:222
  37.8 39.4 %collective-permute-start.1 = (bf16[16,16,16,128]{3,2,1,0:T(8,128)(2,1)}, bf16[16,16,16,128]{3,2,1,0:T(8,128)(2,1)}, u32[]{:S(2)}, u32[]{:S(2)}) collective-permute-start(bf16[16,16,16,128]{3,2,1,0:T(8,128)(2,1)} %get-tuple-element.18.a_ref.refs_2_), channel_id=1, source_target_pairs={{0,7},{1,0},{2,1},{3,2},{4,3},{5,4},{6,5},{7,6},{8,15},{9,8},{10,9... | collective-permute-start | bytes 3145736 | tf_op jit(solution)/shard_map/ppermute | solution.py:222
  54.7 7.6 %copy-start.1 = (bf16[16,16,16,128]{3,2,1,0:T(8,128)(2,1)}, bf16[16,16,16,128]{3,2,1,0:T(8,128)(2,1)S(1)}, u32[]{:S(2)}) copy-start(bf16[16,16,16,128]{3,2,1,0:T(8,128)(2,1)S(1)} %collective-permute-done.3.refs_6_.refs_5_) | copy-start | bytes 3145732
  54.7 45.0 %collective-permute-start.4 = (bf16[16,16,16,128]{3,2,1,0:T(8,128)(2,1)S(1)}, bf16[16,16,16,128]{3,2,1,0:T(8,128)(2,1)}, u32[]{:S(2)}, u32[]{:S(2)}) collective-permute-start(bf16[16,16,16,128]{3,2,1,0:T(8,128)(2,1)S(1)} %collective-permute-done.3.refs_6_.refs_5_), channel_id=1, source_target_pairs={{0,1},{1,2},{2,3},{3,4},{4,5},{5,6},{6,7},{7,0},{8,9},{9,10},{10,1... | collective-permute-start | bytes 3145736 | tf_op jit(solution)/shard_map/ppermute | solution.py:222
  55.5 6.8 %copy-start = (bf16[16,16,16,128]{3,2,1,0:T(8,128)(2,1)}, bf16[16,16,16,128]{3,2,1,0:T(8,128)(2,1)S(1)}, u32[]{:S(2)}) copy-start(bf16[16,16,16,128]{3,2,1,0:T(8,128)(2,1)S(1)} %collective-permute-done.2.refs_5_.refs_4_) | copy-start | bytes 3145732
  55.5 44.2 %collective-permute-start.5 = (bf16[16,16,16,128]{3,2,1,0:T(8,128)(2,1)S(1)}, bf16[16,16,16,128]{3,2,1,0:T(8,128)(2,1)}, u32[]{:S(2)}, u32[]{:S(2)}) collective-permute-start(bf16[16,16,16,128]{3,2,1,0:T(8,128)(2,1)S(1)} %collective-permute-done.2.refs_5_.refs_4_), channel_id=1, source_target_pairs={{0,7},{1,0},{2,1},{3,2},{4,3},{5,4},{6,5},{7,6},{8,15},{9,8},{10,9... | collective-permute-start | bytes 3145736 | tf_op jit(solution)/shard_map/ppermute | solution.py:222
  77.2 2.0 %copy-start.2 = (bf16[16,16,16,128]{3,2,1,0:T(8,128)(2,1)}, bf16[16,16,16,128]{3,2,1,0:T(8,128)(2,1)S(1)}, u32[]{:S(2)}) copy-start(bf16[16,16,16,128]{3,2,1,0:T(8,128)(2,1)S(1)} %collective-permute-done.a_ref.refs_7_.refs_6_) | copy-start | bytes 3145732
  77.2 43.4 %collective-permute-start.6 = (bf16[16,16,16,128]{3,2,1,0:T(8,128)(2,1)}, bf16[16,16,16,128]{3,2,1,0:T(8,128)(2,1)}, u32[]{:S(2)}, u32[]{:S(2)}) collective-permute-start(bf16[16,16,16,128]{3,2,1,0:T(8,128)(2,1)} %collective-permute-done.1.b_ref.refs_4_.refs_3_), channel_id=1, source_target_pairs={{0,7},{1,0},{2,1},{3,2},{4,3},{5,4},{6,5},{7,6},{8,15},{9,8},{10,9... | collective-permute-start | bytes 3145736 | tf_op jit(solution)/shard_map/ppermute | solution.py:222
  77.3 43.3 %collective-permute-start.7 = (bf16[16,16,16,128]{3,2,1,0:T(8,128)(2,1)S(1)}, bf16[16,16,16,128]{3,2,1,0:T(8,128)(2,1)}, u32[]{:S(2)}, u32[]{:S(2)}) collective-permute-start(bf16[16,16,16,128]{3,2,1,0:T(8,128)(2,1)S(1)} %collective-permute-done.a_ref.refs_7_.refs_6_), channel_id=1, source_target_pairs={{0,1},{1,2},{2,3},{3,4},{4,5},{5,6},{6,7},{7,0},{8,9},{9,10},{10,1... | collective-permute-start | bytes 3145736 | tf_op jit(solution)/shard_map/ppermute | solution.py:222
  148.2 10.3 %collective-permute-start.8 = (f32[64,128]{1,0:T(8,128)S(1)}, f32[64,128]{1,0:T(8,128)S(1)}, u32[]{:S(2)}, u32[]{:S(2)}) collective-permute-start(f32[64,128]{1,0:T(8,128)S(1)} %get-tuple-element.31), channel_id=1, source_target_pairs={{0,0},{1,33},{2,66},{3,99},{4,132},{5,165},{6,198},{7,231},{8,32},... | collective-permute-start | bytes 98312 | tf_op jit(solution)/shard_map/ppermute | solution.py:222
  152.3 11.4 %collective-permute-start.9 = (f32[64,128]{1,0:T(8,128)S(1)}, f32[64,128]{1,0:T(8,128)S(1)}, u32[]{:S(2)}, u32[]{:S(2)}) collective-permute-start(f32[64,128]{1,0:T(8,128)S(1)} %get-tuple-element.32), channel_id=1, source_target_pairs={{0,0},{1,33},{2,66},{3,99},{4,132},{5,165},{6,198},{7,231},{8,32},... | collective-permute-start | bytes 98312 | tf_op jit(solution)/shard_map/ppermute | solution.py:222

commit v4 on v3

--- a/solution.py
+++ b/solution.py
@@ -59,8 +59,8 @@
         occ, virt = occ_list[y * 64 + n], virt_list[y * 64 + n]
         occ_here = (((occ >> 3) & 7) == place).astype(F32)
         virt_here = (((virt >> 3) & 7) == place).astype(F32)
-        occ_block = c_ref[(occ >> 6) * 8 + (occ & 7)].astype(F32) * occ_here
-        virt_block = c_ref[(virt >> 6) * 8 + (virt & 7)].astype(F32) * virt_here
+        occ_block = c_ref[((y - (occ >> 6)) & 3) * 8 + (occ & 7)].astype(F32) * occ_here
+        virt_block = c_ref[((y - (virt >> 6)) & 3) * 8 + (virt & 7)].astype(F32) * virt_here
         o_ref[n] = jnp.where(left, occ_block, virt_block).astype(BF16)
         return carry
 
@@ -253,11 +253,15 @@
     both = jnp.concatenate([occ_blocks[0], virt_blocks[0]], axis=1)
     own = order_rows(three_centre[0])
     column = spread(both, "z", 8)
+    own, column = lax.optimization_barrier((own, column))
     below_first, above_first = up(own[0]), down(own[1])
     below_last, above_last = up(own[1]), down(own[0])
     far_below_first, far_above_first = up(below_first), down(above_first)
 
-    held = spread(column, "y", 4).reshape(32, B, 2 * B)
+    held = [column]
+    for n in range(1, 4):
+        held.append(moved(column, lambda y, x, c, z: ((y + n) % 4, x, c, z)))
+    held = jnp.concatenate(held, axis=0)
     chosen = choose(held, occ_list, virt_list)
     arrived = lax.all_to_all(chosen.reshape(8, 8, B, 2 * B), ("x", "c"), 0, 0)
     w1, w2 = term_weights(term_count, arrived)

time: 165 us -> 160 us (0.970)
  blocking collectives: 38 us -> 21 us
  starting transfers between devices: 27.5 us -> 35.1 us
  waiting for transfers between devices: 25.3 us -> 30.1 us
    all_to_all x1 -> x0, blocking collectives: 17.4 us -> none  [spread(): lax.all_to_all(jnp.broadcast_to(block[None], (count,) + block.shape), axi...]
    all_to_all x1, waiting for transfers between devices: 0.01 us -> 5.87 us  [spread(): lax.all_to_all(jnp.broadcast_to(block[None], (count,) + block.shape), axi...]
    ppermute x10 -> x13, starting transfers between devices: 17.9 us -> 21.8 us  [moved(): lax.ppermute(value, ALL, [(number(*p), number(*target(*p))) for p in plac...]
    all_to_all x1, starting transfers between devices: 4.8 us -> 8.47 us  [spread(): lax.all_to_all(jnp.broadcast_to(block[None], (count,) + block.shape), axi...]
    ppermute x10 -> x13, waiting for transfers between devices: 25.3 us -> 24.2 us  [moved(): lax.ppermute(value, ALL, [(number(*p), number(*target(*p))) for p in plac...]
  transfers between devices with their start and end apart: 12 -> 15, of which waited for: 5 -> 8; matrix products, arithmetic and copies ran while one was open for 0% -> 1% of each run, Pallas kernels for 39% -> 40%
where the time goes in v4:
time: 160 us; the launch traced here: 159 us
  Pallas kernels  70.1 us (44%)
  starting transfers between devices  35.1 us (22%)
  waiting for transfers between devices  30.1 us (19%)
  blocking collectives  21 us (13%)
  other arithmetic  2.49 us (2%)
    pallas_call x3, Pallas kernels, image_rows(): pl.pallas_call(image_kernel, grid=(4,), in_specs=[spec, spec, pl.BlockSpe...  37.9 us
    ppermute x13, waiting for transfers between devices, moved(): lax.ppermute(value, ALL, [(number(*p), number(*target(*p))) for p in plac...  24.2 us
    pallas_call x3, Pallas kernels, tiles(): pl.pallas_call(kernel, grid=(4,), in_specs=[pl.BlockSpec((256, 1024), lam...  21.9 us
    ppermute x13, starting transfers between devices, moved(): lax.ppermute(value, ALL, [(number(*p), number(*target(*p))) for p in plac...  21.8 us
    all_to_all x1, blocking collectives, add_up(): arrived = lax.all_to_all(pieces.reshape(32, 2 * B, 128), ORB, 0, 0)  21 us
    all_to_all x1, starting transfers between devices, spread(): lax.all_to_all(jnp.broadcast_to(block[None], (count,) + block.shape), axi...  8.47 us
    all_to_all x1, waiting for transfers between devices, spread(): lax.all_to_all(jnp.broadcast_to(block[None], (count,) + block.shape), axi...  5.87 us
    all_to_all x1, starting transfers between devices, body(): arrived = lax.all_to_all(chosen.reshape(8, 8, B, 2 * B), ('x', 'c'), 0, 0)  4.8 us
  transfers between devices with their start and end apart: 15, of which 8 were waited for; matrix products, arithmetic and copies ran while one was open for 1% of the time, Pallas kernels for 40%

profile of v4, /device:TPU:20, one launch (start us, length us, event | category | flops | bytes accessed | tf_op | source)
XLA Modules:
  0.0 159.4 jit_solution(17789029567325051202)
XLA Ops:
  0.0 0.8 pad_maximum_fusion.1
  1.5 8.5 %all-to-all-start = ((bf16[8,64,128]{2,1,0:T(8,128)(2,1)}), bf16[8,64,128]{2,1,0:T(8,128)(2,1)S(1)}, u32[]{:S(2)}, u32[]{:S(2)}) async-start(bf16[8,64,128]{2,1,0:T(8,128)(2,1)} %broadcast_in_dim.2), calls=%async_computation | async-start | bytes 262144 | tf_op jit(solution)/shard_map/all_to_all | solution.py:234
  9.9 3.2 %shard_map.64 = (bf16[16,16,16,128]{3,2,1,0:T(8,128)(2,1)}, bf16[16,16,16,128]{3,2,1,0:T(8,128)(2,1)}) custom-call(bf16[256,4096]{1,0:T(8,128)(2,1)} %bitcast.8), custom_call_target="tpu_custom_call" | custom-call | flops 536870912 | bytes 4194304 | tf_op jit(solution)/shard_map/pallas_call | solution.py:43
  13.2 5.9 %all-to-all-done = bf16[8,64,128]{2,1,0:T(8,128)(2,1)S(1)} async-done(((bf16[8,64,128]{2,1,0:T(8,128)(2,1)}), bf16[8,64,128]{2,1,0:T(8,128)(2,1)S(1)}, u32[]{:S(2)}, u32[]{:S(2)}) %all-to-all-start) | async-done | bytes 131104 | tf_op jit(solution)/shard_map/all_to_all | solution.py:234
  19.0 1.3 collective-permute-start
  21.0 1.1 collective-permute-start.2
  22.0 2.0 %collective-permute-start.6 = (bf16[16,16,16,128]{3,2,1,0:T(8,128)(2,1)}, bf16[16,16,16,128]{3,2,1,0:T(8,128)(2,1)S(1)}, u32[]{:S(2)}, u32[]{:S(2)}) collective-permute-start(bf16[16,16,16,128]{3,2,1,0:T(8,128)(2,1)} %get-tuple-element.23.a_ref.refs_2_), channel_id=1, source_target_pairs={{0,1},{1,2},{2,3},{3,4},{4,5},{5,6},{6,7},{7,0},{8,9},{9,10},{10,1... | collective-permute-start | bytes 3145736 | tf_op jit(solution)/shard_map/ppermute | solution.py:222
  24.0 1.2 collective-permute-done
  25.2 1.6 collective-permute-done.1
  26.8 0.7 collective-permute-done.2
  27.5 0.9 pad_maximum_fusion.c_ref
  28.4 2.7 %shard_map.65 = bf16[64,64,128]{2,1,0:T(8,128)(2,1)} custom-call(s32[256]{0:T(256)} %occ_list.1, s32[256]{0:T(256)} %virt_list.1, bf16[32,64,128]{2,1,0:T(8,128)(2,1)} %pad_maximum_fusion.c_ref), custom_call_target="tpu_custom_call" | custom-call | flops 2013265920 | bytes 1572864 | tf_op jit(solution)/shard_map/pallas_call | solution.py:74
  31.1 4.8 %all-to-all-start.1 = ((bf16[8,8,64,128]{3,2,1,0:T(8,128)(2,1)}), bf16[8,8,64,128]{3,2,1,0:T(8,128)(2,1)}, u32[]{:S(2)}, u32[]{:S(2)}) async-start(bf16[8,8,64,128]{3,2,1,0:T(8,128)(2,1)} %bitcast.9), calls=%async_computation.1 | async-start | bytes 2097152 | tf_op jit(solution)/shard_map/all_to_all | solution.py:266
  36.5 2.7 %collective-permute-start.4 = (bf16[16,16,16,128]{3,2,1,0:T(8,128)(2,1)}, bf16[16,16,16,128]{3,2,1,0:T(8,128)(2,1)}, u32[]{:S(2)}, u32[]{:S(2)}) collective-permute-start(bf16[16,16,16,128]{3,2,1,0:T(8,128)(2,1)} %get-tuple-element.23.a_ref.refs_2_), channel_id=1, source_target_pairs={{0,7},{1,0},{2,1},{3,2},{4,3},{5,4},{6,5},{7,6},{8,15},{9,8},{10,9... | collective-permute-start | bytes 3145736 | tf_op jit(solution)/shard_map/ppermute | solution.py:222
  39.1 10.4 %collective-permute-done.6.refs_6_.refs_5_ = bf16[16,16,16,128]{3,2,1,0:T(8,128)(2,1)S(1)} collective-permute-done((bf16[16,16,16,128]{3,2,1,0:T(8,128)(2,1)}, bf16[16,16,16,128]{3,2,1,0:T(8,128)(2,1)S(1)}, u32[]{:S(2)}, u32[]{:S(2)}) %collective-permute-start.6) | collective-permute-done | bytes 1048608 | tf_op jit(solution)/shard_map/ppermute | solution.py:222
  49.5 0.8 collective-permute-start.7
  50.4 2.4 %collective-permute-start.8 = (bf16[16,16,16,128]{3,2,1,0:T(8,128)(2,1)S(1)}, bf16[16,16,16,128]{3,2,1,0:T(8,128)(2,1)}, u32[]{:S(2)}, u32[]{:S(2)}) collective-permute-start(bf16[16,16,16,128]{3,2,1,0:T(8,128)(2,1)S(1)} %collective-permute-done.5.refs_5_.refs_4_), channel_id=1, source_target_pairs={{0,7},{1,0},{2,1},{3,2},{4,3},{5,4},{6,5},{7,6},{8,15},{9,8},{10,9... | collective-permute-start | bytes 3145736 | tf_op jit(solution)/shard_map/ppermute | solution.py:222
  52.8 4.4 %shard_map.66 = (bf16[16,8,16,256]{3,2,1,0:T(8,128)(2,1)}, bf16[256,2048]{1,0:T(8,128)(2,1)}) custom-call(s32[32]{0:T(128)} %count_ref.1, bf16[8,8,64,128]{3,2,1,0:T(8,128)(2,1)} %all-to-all-done.1.b_ref), custom_call_target="tpu_custom_call" | custom-call | flops 3355443200 | bytes 3145728 | tf_op jit(solution)/shard_map/pallas_call | solution.py:113
  57.1 12.6 %shard_map.67.refs_0_ = bf16[256,4096]{1,0:T(8,128)(2,1)} custom-call(bf16[16,16,16,128]{3,2,1,0:T(8,128)(2,1)} %get-tuple-element.23.a_ref.refs_2_, bf16[16,16,16,128]{3,2,1,0:T(8,128)(2,1)} %get-tuple-element.24.b_ref.refs_3_, bf16[16,8,16,256]{3,2,1,0:T(8,128)(2,1)} %get-tuple-element.26.w1_ref, bf16[256,2048]{1,0:T(8,128)(2,1)} %get-tuple-element.27.w2_ref), custom_call_target="tpu_custom_call" | custom-call | flops 8589934592 | bytes 6291456 | tf_op jit(solution)/shard_map/pallas_call | solution.py:146
  69.8 2.2 %collective-permute-done.3.a_ref.refs_7_.refs_6_ = bf16[16,16,16,128]{3,2,1,0:T(8,128)(2,1)S(1)} collective-permute-done((bf16[16,16,16,128]{3,2,1,0:T(8,128)(2,1)}, bf16[16,16,16,128]{3,2,1,0:T(8,128)(2,1)S(1)}, u32[]{:S(2)}, u32[]{:S(2)}) %collective-permute-start.3) | collective-permute-done | bytes 1048608 | tf_op jit(solution)/shard_map/ppermute | solution.py:222
  72.0 0.8 collective-permute-start.10
  72.8 2.4 %collective-permute-start.9 = (bf16[16,16,16,128]{3,2,1,0:T(8,128)(2,1)}, bf16[16,16,16,128]{3,2,1,0:T(8,128)(2,1)}, u32[]{:S(2)}, u32[]{:S(2)}) collective-permute-start(bf16[16,16,16,128]{3,2,1,0:T(8,128)(2,1)} %collective-permute-done.4.b_ref.refs_4_.refs_3_), channel_id=1, source_target_pairs={{0,7},{1,0},{2,1},{3,2},{4,3},{5,4},{6,5},{7,6},{8,15},{9,8},{10,9... | collective-permute-start | bytes 3145736 | tf_op jit(solution)/shard_map/ppermute | solution.py:222
  75.3 12.6 %shard_map.68.refs_1_ = bf16[256,4096]{1,0:T(8,128)(2,1)} custom-call(bf16[16,16,16,128]{3,2,1,0:T(8,128)(2,1)} %copy-done.2, bf16[16,16,16,128]{3,2,1,0:T(8,128)(2,1)} %collective-permute-done.4.b_ref.refs_4_.refs_3_, bf16[16,8,16,256]{3,2,1,0:T(8,128)(2,1)} %get-tuple-element.26.w1_ref, bf16[256,2048]{1,0:T(8,128)(2,1)} %get-tuple-element.27.w2_ref), custom_call_target="tpu_custom_call" | custom-call | flops 8589934592 | bytes 6291456 | tf_op jit(solution)/shard_map/pallas_call | solution.py:146
  87.9 7.0 %shard_map.69.refs_9_ = bf16[4,4,2,128,128]{4,3,2,1,0:T(8,128)(2,1)} custom-call(bf16[256,4096]{1,0:T(8,128)(2,1)} %shard_map.67.refs_0_, bf16[256,4096]{1,0:T(8,128)(2,1)} %shard_map.68.refs_1_, bf16[16,16,16,128]{3,2,1,0:T(8,128)(2,1)} %get-tuple-element.23.a_ref.refs_2_, bf16[16,16,16,128]{3,2,1,0:T(8,128)(2,1)} %get-tuple-element.24.b_ref.refs_3_, ...), custom_call_target="tpu_custom_call" | custom-call | flops 2147483648 | bytes 12582912 | tf_op jit(solution)/shard_map/pallas_call | solution.py:196
  94.9 12.6 %shard_map.70.refs_2_ = bf16[256,4096]{1,0:T(8,128)(2,1)} custom-call(bf16[16,16,16,128]{3,2,1,0:T(8,128)(2,1)} %collective-permute-done.7.a_ref.refs_8_, bf16[16,16,16,128]{3,2,1,0:T(8,128)(2,1)} %collective-permute-done.8.b_ref.refs_7_, bf16[16,8,16,256]{3,2,1,0:T(8,128)(2,1)} %get-tuple-element.26.w1_ref, bf16[256,2048]{1,0:T(8,128)(2,1)} %get-tuple-element.27.w2_ref), custom_call_target="tpu_custom_call" | custom-call | flops 8589934592 | bytes 6291456 | tf_op jit(solution)/shard_map/pallas_call | solution.py:146
  107.5 8.2 %shard_map.71.refs_5_ = bf16[4,4,2,128,128]{4,3,2,1,0:T(8,128)(2,1)} custom-call(bf16[256,4096]{1,0:T(8,128)(2,1)} %shard_map.67.refs_0_, bf16[256,4096]{1,0:T(8,128)(2,1)} %shard_map.68.refs_1_, bf16[256,4096]{1,0:T(8,128)(2,1)} %shard_map.70.refs_2_, bf16[16,16,16,128]{3,2,1,0:T(8,128)(2,1)} %collective-permute-done.4.b_ref.refs_4_.refs_3_, ...), custom_call_target="tpu_custom_call" | custom-call | flops 1342177280 | bytes 14680064 | tf_op jit(solution)/shard_map/pallas_call | solution.py:196
  115.7 6.8 %shard_map.72 = bf16[4,4,2,128,128]{4,3,2,1,0:T(8,128)(2,1)} custom-call(bf16[256,4096]{1,0:T(8,128)(2,1)} %shard_map.67.refs_0_, bf16[256,4096]{1,0:T(8,128)(2,1)} %shard_map.68.refs_1_, bf16[256,4096]{1,0:T(8,128)(2,1)} %shard_map.70.refs_2_, bf16[16,16,16,128]{3,2,1,0:T(8,128)(2,1)} %collective-permute-done.9.refs_3_, ...), custom_call_target="tpu_custom_call" | custom-call | flops 805306368 | bytes 10485760 | tf_op jit(solution)/shard_map/pallas_call | solution.py:196
  122.5 21.0 %all_to_all.15 = bf16[32,128,128]{2,1,0:T(8,128)(2,1)S(1)} all-to-all(bf16[32,128,128]{2,1,0:T(8,128)(2,1)} %bitcast.7), channel_id=1, replica_groups=mesh['y'=4,'x'=4,'c'=2,'z'=8] {'y','x','c'}, dimensions={0} | all-to-all | bytes 2097152 | tf_op jit(solution)/shard_map/all_to_all | solution.py:238
  143.6 3.8 %collective-permute-start.11 = (f32[64,128]{1,0:T(8,128)S(1)}, f32[64,128]{1,0:T(8,128)S(1)}, u32[]{:S(2)}, u32[]{:S(2)}) collective-permute-start(f32[64,128]{1,0:T(8,128)S(1)} %get-tuple-element.37), channel_id=1, source_target_pairs={{0,0},{1,33},{2,66},{3,99},{4,132},{5,165},{6,198},{7,231},{8,32},... | collective-permute-start | bytes 98312 | tf_op jit(solution)/shard_map/ppermute | solution.py:222
  147.4 3.3 %collective-permute-start.12 = (f32[64,128]{1,0:T(8,128)S(1)}, f32[64,128]{1,0:T(8,128)S(1)}, u32[]{:S(2)}, u32[]{:S(2)}) collective-permute-start(f32[64,128]{1,0:T(8,128)S(1)} %get-tuple-element.38), channel_id=1, source_target_pairs={{0,0},{1,33},{2,66},{3,99},{4,132},{5,165},{6,198},{7,231},{8,32},... | collective-permute-start | bytes 98312 | tf_op jit(solution)/shard_map/ppermute | solution.py:222
  150.8 3.2 %collective-permute-done.11 = f32[64,128]{1,0:T(8,128)S(1)} collective-permute-done((f32[64,128]{1,0:T(8,128)S(1)}, f32[64,128]{1,0:T(8,128)S(1)}, u32[]{:S(2)}, u32[]{:S(2)}) %collective-permute-start.11) | collective-permute-done | bytes 32800 | tf_op jit(solution)/shard_map/ppermute | solution.py:222
  153.9 4.9 %collective-permute-done.12 = f32[64,128]{1,0:T(8,128)S(1)} collective-permute-done((f32[64,128]{1,0:T(8,128)S(1)}, f32[64,128]{1,0:T(8,128)S(1)}, u32[]{:S(2)}, u32[]{:S(2)}) %collective-permute-start.12) | collective-permute-done | bytes 32800 | tf_op jit(solution)/shard_map/ppermute | solution.py:222
  (21 shorter events, 2.7 us)
Async XLA Ops:
  1.5 17.6 %all-to-all-start = ((bf16[8,64,128]{2,1,0:T(8,128)(2,1)}), bf16[8,64,128]{2,1,0:T(8,128)(2,1)S(1)}, u32[]{:S(2)}, u32[]{:S(2)}) async-start(bf16[8,64,128]{2,1,0:T(8,128)(2,1)} %broadcast_in_dim.2), calls=%async_computation | async-start | bytes 262144 | tf_op jit(solution)/shard_map/all_to_all | solution.py:234
  19.0 6.2 %collective-permute-start = (bf16[8,64,128]{2,1,0:T(8,128)(2,1)S(1)}, bf16[8,64,128]{2,1,0:T(8,128)(2,1)S(1)}, u32[]{:S(2)}, u32[]{:S(2)}) collective-permute-start(bf16[8,64,128]{2,1,0:T(8,128)(2,1)S(1)} %all-to-all-done), channel_id=1, source_target_pairs={{0,64},{1,65},{2,66},{3,67},{4,68},{5,69},{6,70},{7,71},{8,72},{9,... | collective-permute-start | bytes 393224 | tf_op jit(solution)/shard_map/ppermute | solution.py:222
  20.3 6.5 %collective-permute-start.1 = (bf16[8,64,128]{2,1,0:T(8,128)(2,1)S(1)}, bf16[8,64,128]{2,1,0:T(8,128)(2,1)S(1)}, u32[]{:S(2)}, u32[]{:S(2)}) collective-permute-start(bf16[8,64,128]{2,1,0:T(8,128)(2,1)S(1)} %all-to-all-done), channel_id=1, source_target_pairs={{0,128},{1,129},{2,130},{3,131},{4,132},{5,133},{6,134},{7,135},{8... | collective-permute-start | bytes 393224 | tf_op jit(solution)/shard_map/ppermute | solution.py:222
  21.0 6.6 %collective-permute-start.2 = (bf16[8,64,128]{2,1,0:T(8,128)(2,1)S(1)}, bf16[8,64,128]{2,1,0:T(8,128)(2,1)S(1)}, u32[]{:S(2)}, u32[]{:S(2)}) collective-permute-start(bf16[8,64,128]{2,1,0:T(8,128)(2,1)S(1)} %all-to-all-done), channel_id=1, source_target_pairs={{0,192},{1,193},{2,194},{3,195},{4,196},{5,197},{6,198},{7,199},{8... | collective-permute-start | bytes 393224 | tf_op jit(solution)/shard_map/ppermute | solution.py:222
  22.0 28.3 %collective-permute-start.5 = (bf16[16,16,16,128]{3,2,1,0:T(8,128)(2,1)}, bf16[16,16,16,128]{3,2,1,0:T(8,128)(2,1)S(1)}, u32[]{:S(2)}, u32[]{:S(2)}) collective-permute-start(bf16[16,16,16,128]{3,2,1,0:T(8,128)(2,1)} %get-tuple-element.24.b_ref.refs_3_), channel_id=1, source_target_pairs={{0,7},{1,0},{2,1},{3,2},{4,3},{5,4},{6,5},{7,6},{8,15},{9,8},{10,9... | collective-permute-start | bytes 3145736 | tf_op jit(solution)/shard_map/ppermute | solution.py:222
  22.0 27.5 %collective-permute-start.6 = (bf16[16,16,16,128]{3,2,1,0:T(8,128)(2,1)}, bf16[16,16,16,128]{3,2,1,0:T(8,128)(2,1)S(1)}, u32[]{:S(2)}, u32[]{:S(2)}) collective-permute-start(bf16[16,16,16,128]{3,2,1,0:T(8,128)(2,1)} %get-tuple-element.23.a_ref.refs_2_), channel_id=1, source_target_pairs={{0,1},{1,2},{2,3},{3,4},{4,5},{5,6},{6,7},{7,0},{8,9},{9,10},{10,1... | collective-permute-start | bytes 3145736 | tf_op jit(solution)/shard_map/ppermute | solution.py:222
  31.1 21.7 %all-to-all-start.1 = ((bf16[8,8,64,128]{3,2,1,0:T(8,128)(2,1)}), bf16[8,8,64,128]{3,2,1,0:T(8,128)(2,1)}, u32[]{:S(2)}, u32[]{:S(2)}) async-start(bf16[8,8,64,128]{3,2,1,0:T(8,128)(2,1)} %bitcast.9), calls=%async_computation.1 | async-start | bytes 2097152 | tf_op jit(solution)/shard_map/all_to_all | solution.py:266
  35.9 36.1 %collective-permute-start.3 = (bf16[16,16,16,128]{3,2,1,0:T(8,128)(2,1)}, bf16[16,16,16,128]{3,2,1,0:T(8,128)(2,1)S(1)}, u32[]{:S(2)}, u32[]{:S(2)}) collective-permute-start(bf16[16,16,16,128]{3,2,1,0:T(8,128)(2,1)} %get-tuple-element.24.b_ref.refs_3_), channel_id=1, source_target_pairs={{0,1},{1,2},{2,3},{3,4},{4,5},{5,6},{6,7},{7,0},{8,9},{9,10},{10,1... | collective-permute-start | bytes 3145736 | tf_op jit(solution)/shard_map/ppermute | solution.py:222
  36.5 35.6 %collective-permute-start.4 = (bf16[16,16,16,128]{3,2,1,0:T(8,128)(2,1)}, bf16[16,16,16,128]{3,2,1,0:T(8,128)(2,1)}, u32[]{:S(2)}, u32[]{:S(2)}) collective-permute-start(bf16[16,16,16,128]{3,2,1,0:T(8,128)(2,1)} %get-tuple-element.23.a_ref.refs_2_), channel_id=1, source_target_pairs={{0,7},{1,0},{2,1},{3,2},{4,3},{5,4},{6,5},{7,6},{8,15},{9,8},{10,9... | collective-permute-start | bytes 3145736 | tf_op jit(solution)/shard_map/ppermute | solution.py:222
  49.5 7.6 %copy-start.1 = (bf16[16,16,16,128]{3,2,1,0:T(8,128)(2,1)}, bf16[16,16,16,128]{3,2,1,0:T(8,128)(2,1)S(1)}, u32[]{:S(2)}) copy-start(bf16[16,16,16,128]{3,2,1,0:T(8,128)(2,1)S(1)} %collective-permute-done.6.refs_6_.refs_5_) | copy-start | bytes 3145732
  49.5 45.3 %collective-permute-start.7 = (bf16[16,16,16,128]{3,2,1,0:T(8,128)(2,1)S(1)}, bf16[16,16,16,128]{3,2,1,0:T(8,128)(2,1)}, u32[]{:S(2)}, u32[]{:S(2)}) collective-permute-start(bf16[16,16,16,128]{3,2,1,0:T(8,128)(2,1)S(1)} %collective-permute-done.6.refs_6_.refs_5_), channel_id=1, source_target_pairs={{0,1},{1,2},{2,3},{3,4},{4,5},{5,6},{6,7},{7,0},{8,9},{9,10},{10,1... | collective-permute-start | bytes 3145736 | tf_op jit(solution)/shard_map/ppermute | solution.py:222
  50.4 6.8 %copy-start = (bf16[16,16,16,128]{3,2,1,0:T(8,128)(2,1)}, bf16[16,16,16,128]{3,2,1,0:T(8,128)(2,1)S(1)}, u32[]{:S(2)}) copy-start(bf16[16,16,16,128]{3,2,1,0:T(8,128)(2,1)S(1)} %collective-permute-done.5.refs_5_.refs_4_) | copy-start | bytes 3145732
  50.4 44.5 %collective-permute-start.8 = (bf16[16,16,16,128]{3,2,1,0:T(8,128)(2,1)S(1)}, bf16[16,16,16,128]{3,2,1,0:T(8,128)(2,1)}, u32[]{:S(2)}, u32[]{:S(2)}) collective-permute-start(bf16[16,16,16,128]{3,2,1,0:T(8,128)(2,1)S(1)} %collective-permute-done.5.refs_5_.refs_4_), channel_id=1, source_target_pairs={{0,7},{1,0},{2,1},{3,2},{4,3},{5,4},{6,5},{7,6},{8,15},{9,8},{10,9... | collective-permute-start | bytes 3145736 | tf_op jit(solution)/shard_map/ppermute | solution.py:222
  72.0 3.2 %copy-start.2 = (bf16[16,16,16,128]{3,2,1,0:T(8,128)(2,1)}, bf16[16,16,16,128]{3,2,1,0:T(8,128)(2,1)S(1)}, u32[]{:S(2)}) copy-start(bf16[16,16,16,128]{3,2,1,0:T(8,128)(2,1)S(1)} %collective-permute-done.3.a_ref.refs_7_.refs_6_) | copy-start | bytes 3145732
  72.0 43.6 %collective-permute-start.10 = (bf16[16,16,16,128]{3,2,1,0:T(8,128)(2,1)S(1)}, bf16[16,16,16,128]{3,2,1,0:T(8,128)(2,1)}, u32[]{:S(2)}, u32[]{:S(2)}) collective-permute-start(bf16[16,16,16,128]{3,2,1,0:T(8,128)(2,1)S(1)} %collective-permute-done.3.a_ref.refs_7_.refs_6_), channel_id=1, source_target_pairs={{0,1},{1,2},{2,3},{3,4},{4,5},{5,6},{6,7},{7,0},{8,9},{9,10},{10,1... | collective-permute-start | bytes 3145736 | tf_op jit(solution)/shard_map/ppermute | solution.py:222
  72.8 42.8 %collective-permute-start.9 = (bf16[16,16,16,128]{3,2,1,0:T(8,128)(2,1)}, bf16[16,16,16,128]{3,2,1,0:T(8,128)(2,1)}, u32[]{:S(2)}, u32[]{:S(2)}) collective-permute-start(bf16[16,16,16,128]{3,2,1,0:T(8,128)(2,1)} %collective-permute-done.4.b_ref.refs_4_.refs_3_), channel_id=1, source_target_pairs={{0,7},{1,0},{2,1},{3,2},{4,3},{5,4},{6,5},{7,6},{8,15},{9,8},{10,9... | collective-permute-start | bytes 3145736 | tf_op jit(solution)/shard_map/ppermute | solution.py:222
  143.6 10.3 %collective-permute-start.11 = (f32[64,128]{1,0:T(8,128)S(1)}, f32[64,128]{1,0:T(8,128)S(1)}, u32[]{:S(2)}, u32[]{:S(2)}) collective-permute-start(f32[64,128]{1,0:T(8,128)S(1)} %get-tuple-element.37), channel_id=1, source_target_pairs={{0,0},{1,33},{2,66},{3,99},{4,132},{5,165},{6,198},{7,231},{8,32},... | collective-permute-start | bytes 98312 | tf_op jit(solution)/shard_map/ppermute | solution.py:222
  147.4 11.4 %collective-permute-start.12 = (f32[64,128]{1,0:T(8,128)S(1)}, f32[64,128]{1,0:T(8,128)S(1)}, u32[]{:S(2)}, u32[]{:S(2)}) collective-permute-start(f32[64,128]{1,0:T(8,128)S(1)} %get-tuple-element.38), channel_id=1, source_target_pairs={{0,0},{1,33},{2,66},{3,99},{4,132},{5,165},{6,198},{7,231},{8,32},... | collective-permute-start | bytes 98312 | tf_op jit(solution)/shard_map/ppermute | solution.py:222
